TPU v7x, 32 devices: a whole 2x2x4 slice. The times are simulated.
32 devices in a mesh: groups: 2 (over x), section: 8 (over z, y), tensor: 2 (over core).
Axes of the slice: x: 2, y: 2, z: 4, core: 2. Of those that a mesh axis runs over, the one named last changes fastest.
Arguments:
- prompt_states: bfloat16 [16384, 8192], P(('groups', 'section')), parts along dimension 0, may hold values from -6 to 6
- norm_gain: bfloat16 [8192], replicated, may hold values from 0.5 to 1.5
- w_kv: bfloat16 [8192, 2, 512], P(None, None, 'tensor'), may hold values from -0.0625 to 0.0625
- pool_cache: bfloat16 [768, 64, 2, 512], P(('groups', 'section'), None, None, 'tensor'), parts along dimension 0, may hold values from -6 to 6
- queries: bfloat16 [64, 4, 4096], P(('groups', 'section'), None, 'tensor'), parts along dimension 0, may hold values from -110 to 110
- new_kv: bfloat16 [64, 4, 2, 512], P(('groups', 'section'), None, None, 'tensor'), parts along dimension 0, may hold values from -6 to 6
- ship_dest: int32 [256, 1], P('groups'), parts along dimension 0, may hold values from 0 to 7, as said below
- page_row: int32 [256], P('groups'), parts along dimension 0, may hold values from 0 to 3, as said below
- finished: int32 [256], P('groups'), parts along dimension 0, may hold values from 0 to 1, as said below
- page_table: int32 [64, 12], P('groups'), parts along dimension 0, may hold values from 0 to 383, as said below
- row_length: int32 [64], P('groups'), parts along dimension 0, may hold values from 1 to 768, as said below
Outputs:
- attended: bfloat16 [64, 4, 4096], P(('groups', 'section'), None, 'tensor'), parts along dimension 0
There are 2 independent parts, one for each index of `groups`. A program takes and returns all parts, laid end to end along the dimension named above; an argument that names none is the same for every part. Nothing has to cross between parts.
Inputs may be any that keep to these rules, and one draw needn't show every extreme that they name: `page_table`: distinct resident page ids; the largest is reached. `row_length`: the longest row fills all 12 pages. `ship_dest`: the prompt pages of one device form whole prompts, each a run of consecutive pages with one owner, one row and one finished flag; a device hands at most one prompt of at most 3 pages to one owner, and on every device some owner gets exactly 3. `page_row`: equal over the pages of one prompt. `finished`: equal over the pages of one prompt.
All inputs are finite; a program needn't handle non-finite values.
Results may differ from a plain program's by a relative error of at most 0.012.
The roundings to bfloat16 on the way count: a program that leaves them out, or rounds other values in their place, can miss the bound.
Values may be sent and summed in bfloat16 or wider, within the bound.
A program may use at most 128 MiB of HBM per device.

v0:
```python
import math

import jax
import jax.numpy as jnp
from jax import lax
from jax.sharding import PartitionSpec as P

HS = 128
CAP = 3


masked_value = -1e30
norm_epsilon = 1e-05


def page_scores(query_pages, key_pages, live_counts):
    pages_here, steps_here, width_q = query_pages.shape
    page_len = key_pages.shape[1]
    kv_heads = key_pages.shape[2] // HS
    grouped = query_pages.reshape(pages_here, steps_here, kv_heads, width_q // (kv_heads * HS), HS)
    key_heads = key_pages.reshape(pages_here, page_len, kv_heads, HS)
    scores = jnp.einsum(
        "psgqe,ptge->psgqt", grouped, key_heads, preferred_element_type=jnp.float32
    ) * (1.0 / math.sqrt(HS))
    usable = jnp.arange(page_len, dtype=jnp.int32)[None, :] < live_counts[:, None]
    return jnp.where(usable[:, None, None, None, :], scores, masked_value)


def page_terms(scores, tops, value_pages):
    weights = jnp.exp(scores - tops[..., None])
    totals = jnp.sum(weights, axis=-1)
    pages_here, steps_here, kv_heads, group_size, page_len = scores.shape
    value_heads = value_pages.reshape(pages_here, page_len, kv_heads, HS)
    summed = jnp.einsum(
        "psgqt,ptge->psgqe",
        weights.astype(jnp.bfloat16),
        value_heads,
        preferred_element_type=jnp.float32,
    )
    return (summed.reshape(pages_here, steps_here, -1), totals.reshape(pages_here, steps_here, -1))


def body(
    prompt_states,
    norm_gain,
    w_kv,
    pool_cache,
    queries,
    new_kv,
    ship_dest,
    page_row,
    finished,
    page_table,
    row_length,
):
    sections = lax.axis_size("section")
    myself = lax.axis_index("section")
    rows_dev, steps_all, width_q = queries.shape
    pool_pages = pool_cache.shape[0]
    page_len = pool_cache.shape[1]
    width_kv = pool_cache.shape[3]
    kv_heads = width_kv // HS
    group_size = width_q // width_kv
    head_count = width_q // HS
    prompt_pages = prompt_states.shape[0] // page_len
    all_rows = page_table.shape[0]
    max_pages = page_table.shape[1]
    states = prompt_states.astype(jnp.float32)
    spread = lax.rsqrt(jnp.mean(states * states, axis=-1, keepdims=True) + norm_epsilon)
    normed = (states * spread * norm_gain.astype(jnp.float32)).astype(jnp.bfloat16)
    prompt_kv = jnp.einsum("td,dkc->tkc", normed, w_kv, preferred_element_type=jnp.float32).astype(
        jnp.bfloat16
    )
    prompt_kv = prompt_kv.reshape(prompt_pages, page_len, 2, width_kv)
    gathered_q = lax.all_gather(queries, "section", axis=0, tiled=True)
    page_ids = myself * pool_pages + jnp.arange(pool_pages, dtype=jnp.int32)
    page_hits = page_table[:, :, None] == page_ids[None, None, :]
    token_fill = jnp.clip(
        row_length[:, None] - jnp.arange(max_pages, dtype=jnp.int32)[None, :] * page_len,
        0,
        page_len,
    )
    resident_counts = jnp.sum(jnp.where(page_hits, token_fill[:, :, None], 0), axis=(0, 1))
    resident_rows = jnp.sum(
        jnp.where(page_hits, jnp.arange(all_rows, dtype=jnp.int32)[:, None, None], 0), axis=(0, 1)
    )
    dest_grid = ship_dest[:, 0].reshape(sections, prompt_pages)
    done_grid = finished.reshape(sections, prompt_pages)
    bound_for = (dest_grid[:, :, None] == jnp.arange(sections, dtype=jnp.int32)[None, None, :]) & (
        done_grid[:, :, None] == 1
    )
    slot_rank = jnp.cumsum(bound_for.astype(jnp.int32), axis=1) - 1
    slot_grid = jnp.sum(jnp.where(bound_for, slot_rank, 0), axis=-1)
    slot_ids = jnp.arange(CAP, dtype=jnp.int32)
    own_bound = lax.dynamic_index_in_dim(bound_for, myself, 0, keepdims=False)
    own_slots = lax.dynamic_index_in_dim(slot_grid, myself, 0, keepdims=False)
    selector = own_bound.T[:, None, :] & (own_slots[None, None, :] == slot_ids[None, :, None])
    outgoing = jnp.einsum(
        "dcj,jtkw->dctkw",
        selector.astype(jnp.bfloat16),
        prompt_kv,
        preferred_element_type=jnp.float32,
    ).astype(jnp.bfloat16)
    arrived = lax.all_to_all(outgoing, "section", split_axis=0, concat_axis=0, tiled=True)
    toward_me = lax.dynamic_index_in_dim(bound_for, myself, 2, keepdims=False)
    arrival_match = toward_me[:, :, None] & (slot_grid[:, :, None] == slot_ids[None, None, :])
    row_grid = page_row.reshape(sections, prompt_pages)
    arrival_rows = jnp.sum(jnp.where(arrival_match, row_grid[:, :, None], 0), axis=1).reshape(-1)
    arrival_live = jnp.any(arrival_match, axis=1).reshape(-1)
    arrival_kv = arrived.reshape(sections * CAP, page_len, 2, width_kv)
    set_scores = page_scores(gathered_q[resident_rows], pool_cache[:, :, 0], resident_counts)
    set_count = pool_cache.shape[0]
    set_max = jnp.max(set_scores, axis=-1).reshape(set_count, steps_all, head_count)
    row_owner = resident_rows[:, None] == jnp.arange(all_rows, dtype=jnp.int32)[None, :]
    local_max = jnp.max(
        jnp.where(row_owner[:, :, None, None], set_max[:, None], masked_value), axis=0
    )
    own_grouped = queries.reshape(rows_dev, steps_all, kv_heads, group_size, HS)
    fresh_keys = new_kv[:, :, 0].reshape(rows_dev, steps_all, kv_heads, HS)
    fresh_scores = jnp.einsum(
        "rsgqe,ruge->rsgqu", own_grouped, fresh_keys, preferred_element_type=jnp.float32
    ) * (1.0 / math.sqrt(HS))
    step_ids = jnp.arange(steps_all, dtype=jnp.int32)
    causal = step_ids[:, None] >= step_ids[None, :]
    fresh_scores = jnp.where(causal[None, :, None, None, :], fresh_scores, masked_value)
    own_max = jnp.max(fresh_scores, axis=-1).reshape(rows_dev, steps_all, head_count)
    arrival_scores = page_scores(
        queries[arrival_rows], arrival_kv[:, :, 0], arrival_live.astype(jnp.int32) * page_len
    )
    arrival_owner = (
        arrival_rows[:, None] == jnp.arange(rows_dev, dtype=jnp.int32)[None, :]
    ) & arrival_live[:, None]
    arrival_page_max = jnp.max(arrival_scores, axis=-1).reshape(-1, steps_all, head_count)
    arrival_max = jnp.max(
        jnp.where(arrival_owner[:, :, None, None], arrival_page_max[:, None], masked_value), axis=0
    )
    own_max = jnp.maximum(own_max, arrival_max)
    start_row = myself * rows_dev
    mine_max = lax.dynamic_slice_in_dim(local_max, start_row, rows_dev, 0)
    local_max = lax.dynamic_update_slice_in_dim(
        local_max, jnp.maximum(mine_max, own_max), start_row, 0
    )
    row_tops = lax.pmax(local_max, "section")
    set_tops = row_tops[resident_rows].reshape(set_count, steps_all, kv_heads, group_size)
    set_sums, set_totals = page_terms(set_scores, set_tops, pool_cache[:, :, 1])
    owner_float = row_owner.astype(jnp.float32)
    row_sums = jnp.einsum("pr,psc->rsc", owner_float, set_sums, precision=lax.Precision.HIGHEST)
    row_totals = jnp.einsum("pr,psh->rsh", owner_float, set_totals, precision=lax.Precision.HIGHEST)
    own_sums, own_totals = (
        lax.psum_scatter(row_sums, "section", scatter_dimension=0, tiled=True),
        lax.psum_scatter(row_totals, "section", scatter_dimension=0, tiled=True),
    )
    own_tops = lax.dynamic_slice_in_dim(row_tops, start_row, rows_dev, 0)
    fresh_values = new_kv[:, :, 1].reshape(rows_dev, steps_all, kv_heads, HS)
    fresh_weights = jnp.exp(
        fresh_scores - own_tops.reshape(rows_dev, steps_all, kv_heads, group_size)[..., None]
    )
    fresh_sums = jnp.einsum(
        "rsgqu,ruge->rsgqe",
        fresh_weights.astype(jnp.bfloat16),
        fresh_values,
        preferred_element_type=jnp.float32,
    )
    own_sums = own_sums + fresh_sums.reshape(rows_dev, steps_all, width_q)
    own_totals = own_totals + jnp.sum(fresh_weights, axis=-1).reshape(
        rows_dev, steps_all, head_count
    )
    arrival_tops = own_tops[arrival_rows].reshape(-1, steps_all, kv_heads, group_size)
    arrival_sums, arrival_totals = page_terms(arrival_scores, arrival_tops, arrival_kv[:, :, 1])
    arrival_float = arrival_owner.astype(jnp.float32)
    own_sums = own_sums + jnp.einsum(
        "pr,psc->rsc", arrival_float, arrival_sums, precision=lax.Precision.HIGHEST
    )
    own_totals = own_totals + jnp.einsum(
        "pr,psh->rsh", arrival_float, arrival_totals, precision=lax.Precision.HIGHEST
    )
    heads_view = own_sums.reshape(rows_dev, steps_all, head_count, HS) / own_totals[..., None]
    return heads_view.reshape(rows_dev, steps_all, width_q).astype(jnp.bfloat16)


def solution(mesh):
    return jax.shard_map(
        body,
        mesh=mesh,
        in_specs=(
            P(("groups", "section"), None),
            P(),
            P(None, None, "tensor"),
            P(("groups", "section"), None, None, "tensor"),
            P(("groups", "section"), None, "tensor"),
            P(("groups", "section"), None, None, "tensor"),
            P("groups", None),
            P("groups"),
            P("groups"),
            P("groups", None),
            P("groups"),
        ),
        out_specs=P(("groups", "section"), None, "tensor"),
        check_vma=False,
    )
```

profile of v0, /device:TPU:8, one launch (start us, length us, event | category | flops | bytes accessed | tf_op | source)
XLA Modules:
  0.0 273.1 jit_solution(3857393775312626407)
XLA Ops:
  7.0 1.3 reduce.9
  10.2 0.7 convert_element_type.36
  10.9 7.2 %fusion = f32[1024]{0:T(1024)S(1)} fusion(bf16[1024,8192]{1,0:T(8,128)(2,1)} %param.11), kind=kLoop, calls=%fused_computation.6 | loop fusion | flops 25164800 | bytes 16781312 | tf_op jit(solution)/shard_map/reduce_sum | solution.py:69
  18.1 15.0 %fusion.14 = bf16[1024,2,256]{2,0,1:T(8,128)(2,1)S(1)} fusion(bf16[8192,2,256]{2,1,0:T(2,128)(2,1)} %param.13, bf16[1024,8192]{1,0:T(8,128)(2,1)} %param.11, f32[8192]{0:T(1024)S(1)} %convert_element_type.36, f32[1024]{0:T(1024)S(1)} %add_rsqrt_fusion), kind=kOutput, calls=%fused_computation.26 | convolution fusion | flops 8624013312 | bytes 26251264 | tf_op jit(solution)/shard_map/td,dkc->tkc/dot_general | solution.py:71
  33.2 0.8 convolution_convert_fusion
  34.0 2.7 copy.173
  36.7 6.4 %all-to-all-start = ((bf16[8,3,64,2,256]{4,3,2,1,0:T(2,128)(2,1)}), bf16[8,3,64,2,256]{4,3,2,1,0:T(2,128)(2,1)}, u32[]{:S(2)}, u32[]{:S(2)}) async-start(bf16[8,3,64,2,256]{4,3,2,1,0:T(2,128)(2,1)} %copy.173), calls=%async_computation | async-start | bytes 3145728 | tf_op jit(solution)/shard_map/all_to_all | solution.py:104
  44.1 56.2 %all_gather.3 = bf16[32,4,2048]{2,1,0:T(4,128)(2,1)} all-gather(bf16[4,4,2048]{2,1,0:T(4,128)(2,1)S(1)} %copy-done.3), channel_id=1, replica_groups=mesh['groups'=2,'section'=8,'tensor'=2] {'section'}, dimensions={0}, use_global_device_ids=true | all-gather | bytes 589824 | tf_op jit(solution)/shard_map/all_gather | solution.py:75
  100.4 0.9 gather_fusion.1
  101.3 1.0 reshape.299
  102.8 3.3 %gather_fusion = bf16[48,4,2048]{2,1,0:T(4,128)(2,1)} fusion(bf16[32,4,2048]{2,1,0:T(4,128)(2,1)} %all_gather.3, s32[1024]{0:T(1024)S(1)} %pad_clamp_fusion.1), kind=kCustom, calls=%fused_computation | custom fusion | bytes 1573056 | tf_op jit(solution)/shard_map/gather | solution.py:111
  106.1 2.5 reshape.293
  108.7 14.5 %slice_reduce_fusion = (bf16[48,64,256]{2,1,0:T(8,128)(2,1)}, bf16[48,64,256]{2,1,0:T(8,128)(2,1)}) fusion(bf16[48,64,2,256]{3,2,1,0:T(2,128)(2,1)S(1)} %copy-done), kind=kLoop, calls=%fused_computation.12 | loop fusion | bytes 6291456 | tf_op jit(solution)/shard_map/slice | solution.py:145
  123.1 2.4 reshape_squeeze.18
  125.6 3.4 %bitcast_reduce_fusion = (f32[48,4,2,8]{3,1,2,0:T(4,128)S(1)}, f32[48,2,4,8,64]{4,3,2,1,0:T(8,128)}) fusion(bf16[48,64,2,128,1]{3,2,1,0,4:T(2,128)(2,1)S(1)} %bitcast.117, bf16[48,4,2,8,128]{4,3,2,1,0:T(8,128)(2,1)} %reshape.293, pred[48,64]{1,0:T(8,128)(4,1)S(1)} %iota_compare_fusion.1), kind=kOutput, calls=%fused_computation.21 | convolution fusion | flops 50918400 | bytes 3161088 | tf_op jit(solution)/shard_map/psgqe,ptge->psgqt/dot_general | solution.py:22
  129.7 1.0 fusion.79
  132.8 1.0 select_reduce_fusion
  135.0 1.7 copy.174
  136.7 1.1 fusion.76
  137.8 1.1 reshape_squeeze.20
  138.9 3.3 %fusion.80 = (f32[24,4,2,8]{3,1,2,0:T(4,128)}, f32[24,4,2,8,64]{4,3,1,2,0:T(8,128)}) fusion(bf16[24,4,2,8,128]{4,3,2,1,0:T(8,128)(2,1)S(1)} %copy-done.6, bf16[24,64,2,128,1]{3,2,1,0,4:T(2,128)(2,1)} %bitcast.121, pred[24,64]{1,0:T(8,128)(4,1)} %iota_compare_fusion.3), kind=kOutput, calls=%fused_computation.118 | convolution fusion | flops 25459200 | bytes 1580544 | tf_op jit(solution)/shard_map/psgqe,ptge->psgqt/dot_general | solution.py:22
  142.2 1.0 copy.178
  143.2 0.8 select_reduce_fusion.1
  143.9 1.3 maximum_dynamic-update-slice_fusion
  145.3 36.1 %pmax.7 = f32[32,4,16]{2,1,0:T(4,128)S(1)} all-reduce(f32[32,4,16]{2,1,0:T(4,128)} %maximum_dynamic-update-slice_fusion), channel_id=1, replica_groups=mesh['groups'=2,'section'=8,'tensor'=2] {'section'}, use_global_device_ids=true, to_apply=%region_12.13 | all-reduce | flops 2048 | bytes 16384 | tf_op jit(solution)/shard_map/pmax | solution.py:143
  182.3 1.1 fusion.24
  183.4 0.8 fusion.19
  184.6 1.8 fusion.56
  186.4 0.8 gather_fusion.3
  189.6 33.8 %all-reduce.1 = f32[32,4,16]{2,0,1:T(8,128)S(1)} all-reduce(f32[32,4,16]{2,0,1:T(8,128)S(1)} %fusion.52), channel_id=3, replica_groups=mesh['groups'=2,'section'=8,'tensor'=2] {'section'}, use_global_device_ids=true, to_apply=%region_15.16.clone | all-reduce | flops 2048 | bytes 16384
  224.1 40.2 %all-reduce.4.cloned.1.call-done = f32[32,4,2048]{2,0,1:T(8,128)} async-done(((f32[32,4,2048]{2,0,1:T(8,128)}), f32[32,4,2048]{2,0,1:T(8,128)}) %all-reduce.4.cloned.1.call-update) | async-done | bytes 1048592
  264.3 1.3 fusion.8
  (108 shorter events, 12.2 us)
Async XLA Ops:
  36.7 6.8 %copy-start.13 = (s32[128]{0:T(128)S(1)}, s32[128]{0:T(128)}, u32[]{:S(2)}) copy-start(s32[128]{0:T(128)} %param.18) | copy-start | bytes 1540
  36.7 7.4 %copy-start.3 = (bf16[4,4,2048]{2,1,0:T(4,128)(2,1)S(1)}, bf16[4,4,2048]{2,1,0:T(4,128)(2,1)}, u32[]{:S(2)}) copy-start(bf16[4,4,2048]{2,1,0:T(4,128)(2,1)} %param.15) | copy-start | bytes 196612
  36.7 98.4 %all-to-all-start = ((bf16[8,3,64,2,256]{4,3,2,1,0:T(2,128)(2,1)}), bf16[8,3,64,2,256]{4,3,2,1,0:T(2,128)(2,1)}, u32[]{:S(2)}, u32[]{:S(2)}) async-start(bf16[8,3,64,2,256]{4,3,2,1,0:T(2,128)(2,1)} %copy.173), calls=%async_computation | async-start | bytes 3145728 | tf_op jit(solution)/shard_map/all_to_all | solution.py:104
  43.1 59.4 %copy-start.14 = (s32[32]{0:T(128)S(1)}, s32[32]{0:T(128)}, u32[]{:S(2)}) copy-start(s32[32]{0:T(128)} %param.21) | copy-start | bytes 388
  43.1 59.5 %copy-start.10 = (s32[32,12]{0,1:T(8,128)S(1)}, s32[32,12]{0,1:T(8,128)}, u32[]{:S(2)}) copy-start(s32[32,12]{0,1:T(8,128)} %param.20) | copy-start | bytes 4612
  43.1 221.2 %all-reduce.4.cloned.1.call-start = ((), (), s32[]{:S(2)}) async-start(), calls=%async_computation.1 | async-start | bytes 2097152
  100.4 2.4 copy-start.11
  102.8 5.9 %copy-start = (bf16[48,64,2,256]{3,2,1,0:T(2,128)(2,1)S(1)}, bf16[48,64,2,256]{3,2,1,0:T(2,128)(2,1)}, u32[]{:S(2)}) copy-start(bf16[48,64,2,256]{3,2,1,0:T(2,128)(2,1)} %param.14) | copy-start | bytes 9437188
  125.6 3.5 %copy-start.8 = (bf16[4,4,2,256]{3,2,1,0:T(2,128)(2,1)S(1)}, bf16[4,4,2,256]{3,2,1,0:T(2,128)(2,1)}, u32[]{:S(2)}) copy-start(bf16[4,4,2,256]{3,2,1,0:T(2,128)(2,1)} %param.16) | copy-start | bytes 49156
  125.6 5.3 %copy-start.1 = (bf16[48,64,256]{2,1,0:T(8,128)(2,1)S(1)}, bf16[48,64,256]{2,1,0:T(8,128)(2,1)}, u32[]{:S(2)}) copy-start(bf16[48,64,256]{2,1,0:T(8,128)(2,1)} %get-tuple-element.5) | copy-start | bytes 4718596
  130.9 0.7 copy-start.15
  137.8 1.1 copy-start.6
  138.9 43.4 %copy-start.2 = (f32[48,2,4,8,64]{4,3,2,1,0:T(8,128)S(1)}, f32[48,2,4,8,64]{4,3,2,1,0:T(8,128)}, u32[]{:S(2)}) copy-start(f32[48,2,4,8,64]{4,3,2,1,0:T(8,128)} %get-tuple-element.14) | copy-start | bytes 2359300
  184.6 2.8 %copy-start.4 = (bf16[24,64,1,256]{3,1,2,0:T(8,128)(2,1)S(1)}, bf16[24,64,1,256]{3,1,2,0:T(8,128)(2,1)}, u32[]{:S(2)}) copy-start(bf16[24,64,1,256]{3,1,2,0:T(8,128)(2,1)} %get-tuple-element.9) | copy-start | bytes 2359300
  186.4 1.3 copy-start.5
  188.2 1.0 copy-start.7
  188.2 35.2 %copy-start.12 = (pred[24,4]{0,1:T(4,128)(4,1)S(1)}, pred[24,4]{0,1:T(4,128)(4,1)}, u32[]{:S(2)}) copy-start(pred[24,4]{0,1:T(4,128)(4,1)} %fusion.70) | copy-start | bytes 292
  188.2 35.6 %copy-start.9 = (bf16[4,4,1,256]{3,2,1,0:T(2,128)(2,1)S(1)}, bf16[4,4,1,256]{3,2,1,0:T(2,128)(2,1)}, u32[]{:S(2)}) copy-start(bf16[4,4,1,256]{3,2,1,0:T(2,128)(2,1)} %get-tuple-element.11) | copy-start | bytes 24580
Sparse Core Ops, SparseCore 0:
  186.5 77.7 all-reduce.3
where the time goes:
time: 276 us; the launch traced here: 273 us
  blocking collectives  126 us (46%)
  waiting for transfers between devices  40.2 us (15%)
  local copies, waits for them, and re-layouts  40.1 us (15%)
  matrix products  28.5 us (10%)
  other arithmetic  17.3 us (6%)
  between operations  14.5 us (5%)
  starting transfers between devices  6.45 us (2%)
    all_gather x1, blocking collectives, body(): gathered_q = lax.all_gather(queries, 'section', axis=0, tiled=True)  56.2 us
    unnamed x2, waiting for transfers between devices  40.2 us
    pmax x1, blocking collectives, body(): row_tops = lax.pmax(local_max, 'section')  36.1 us
    unnamed x1, blocking collectives  33.8 us
    dot_general x1, matrix products, body(): jnp.einsum('td,dkc->tkc', normed, w_kv, preferred_element_type=jnp.float32)  15 us
    slice x1, local copies, waits for them, and re-layouts, body(): set_sums, set_totals = page_terms(set_scores, set_tops, pool_cache[:, :, 1])  14.5 us
    reduce_sum x1, other arithmetic, body(): jnp.mean(states * states, axis=-1, keepdims=True) + norm_epsilon  7.18 us
    dot_general x2, matrix products, page_scores(): jnp.einsum('psgqe,ptge->psgqt', grouped, key_heads, preferred_element_typ...  6.7 us
  transfers between devices with their start and end apart: 2, of which 1 were waited for; matrix products, arithmetic and copies ran while one was open for 14% of the time, Pallas kernels for 0%

commit v1 on v0

v1 whole, which is shorter than its diff:
```python
import functools
import math

import jax
import jax.numpy as jnp
from jax import lax
from jax.experimental import pallas as pl
from jax.experimental.pallas import tpu as pltpu
from jax.sharding import PartitionSpec as P

HS = 128
MESH = pl.DeviceIdType.MESH
masked_value = -1e30
norm_epsilon = 1e-05
VMEM_LIMIT = 48 * 1024 * 1024
UNROLL = 4


def vmem():
    return pl.BlockSpec(memory_space=pltpu.VMEM)


def smem():
    return pl.BlockSpec(memory_space=pltpu.SMEM)


def greet(n, me):
    barrier = pltpu.get_barrier_semaphore()
    for k in range(1, n):
        pl.semaphore_signal(
            barrier, inc=1, device_id={"section": lax.rem(me + k, n)}, device_id_type=MESH
        )
    pl.semaphore_wait(barrier, n - 1)


def gather_kernel(n, own_ref, all_ref, send_sem, recv_sem):
    me = lax.axis_index("section")
    greet(n, me)
    copies = []
    for k in range(1, n):
        copy = pltpu.make_async_remote_copy(
            src_ref=own_ref,
            dst_ref=all_ref.at[me],
            send_sem=send_sem.at[k],
            recv_sem=recv_sem.at[k],
            device_id={"section": lax.rem(me + k, n)},
            device_id_type=MESH,
        )
        copy.start()
        copies.append(copy)
    all_ref[me] = own_ref[...]
    for copy in copies:
        copy.wait()


def attend_kernel(
    rows_dev, n, rows_ref, counts_ref, q_ref, pool_k, pool_v, prompt_k, prompt_v, fresh_k, fresh_v,
    out_ref, ml_ref, acc, tops, totals,
):
    span = q_ref.shape[0] // (n * rows_dev)
    half = span // 2
    page_len = 64
    pool_pages = pool_k.shape[0] // page_len
    prompt_pages = prompt_k.shape[0] // page_len
    scale = 1.0 / math.sqrt(HS)
    acc[...] = jnp.zeros_like(acc)
    totals[...] = jnp.zeros_like(totals)
    tops[...] = jnp.full_like(tops, masked_value)
    token = lax.broadcasted_iota(jnp.int32, (span, page_len), 1)
    line = lax.broadcasted_iota(jnp.int32, (span, page_len), 0)
    step = lax.rem(line, half) // 8
    contract_last = (((1,), (1,)), ((), ()))

    def page_part(row, count, keys, values, at, causal):
        q = q_ref[pl.ds(pl.multiple_of(row * span, span), span), :]
        k = keys[pl.ds(pl.multiple_of(at * page_len, page_len), page_len), :]
        v = values[pl.ds(pl.multiple_of(at * page_len, page_len), page_len), :]
        low = lax.dot_general(
            q[:half], k[:, :HS], contract_last, preferred_element_type=jnp.float32
        )
        high = lax.dot_general(
            q[half:], k[:, HS:], contract_last, preferred_element_type=jnp.float32
        )
        scores = jnp.concatenate([low, high], axis=0) * scale
        usable = (token <= step) if causal else (token < count)
        scores = jnp.where(usable, scores, masked_value)
        top = jnp.max(scores, axis=1, keepdims=True)
        weights = jnp.where(usable, jnp.exp(scores - top), 0.0)
        total = jnp.sum(weights, axis=1, keepdims=True)
        main = weights.astype(jnp.bfloat16)
        rest = (weights - main.astype(jnp.float32)).astype(jnp.bfloat16)
        both_low = jnp.concatenate([main[:half], rest[:half]], axis=0)
        both_high = jnp.concatenate([main[half:], rest[half:]], axis=0)
        sum_low = jnp.dot(both_low, v[:, :HS], preferred_element_type=jnp.float32)
        sum_high = jnp.dot(both_high, v[:, HS:], preferred_element_type=jnp.float32)
        summed = jnp.concatenate(
            [sum_low[:half] + sum_low[half:], sum_high[:half] + sum_high[half:]], axis=0
        )
        return top, total, summed

    def update(row, part):
        top, total, summed = part
        place = pl.ds(pl.multiple_of(row * span, span), span)
        old = tops[place, :]
        new = jnp.maximum(old, top)
        keep = jnp.exp(old - new)
        add = jnp.exp(top - new)
        tops[place, :] = new
        totals[place, :] = totals[place, :] * keep + total * add
        acc[place, :] = acc[place, :] * keep + summed * add

    def run(first, pages, keys, values, causal):
        def some(i, _):
            parts = []
            for u in range(UNROLL):
                at = i * UNROLL + u
                row = rows_ref[first + at]
                parts.append((row, page_part(row, counts_ref[first + at], keys, values, at, causal)))
            for row, part in parts:
                update(row, part)
            return 0

        lax.fori_loop(0, pages // UNROLL, some, 0)

    run(0, pool_pages, pool_k, pool_v, False)
    run(pool_pages, prompt_pages, prompt_k, prompt_v, False)
    run(pool_pages + prompt_pages, rows_dev, fresh_k, fresh_v, True)

    block = rows_dev * span
    lane = lax.broadcasted_iota(jnp.int32, (block, HS), 1)
    for d in range(n):
        here = pl.ds(d * block, block)
        out_ref[d] = acc[here, :].astype(jnp.bfloat16)
        mixed = jnp.where(lane == 0, tops[here, :], totals[here, :])
        ml_ref[d] = mixed.T[:8, :]


def merge_kernel(n, part_ref, ml_ref, out_ref, parts, mls, coef, send_sem, recv_sem):
    me = lax.axis_index("section")
    greet(n, me)
    copies = []
    for k in range(1, n):
        to = lax.rem(me + k, n)
        for which, (src, dst) in enumerate(((part_ref, parts), (ml_ref, mls))):
            copy = pltpu.make_async_remote_copy(
                src_ref=src.at[to],
                dst_ref=dst.at[me],
                send_sem=send_sem.at[which, k],
                recv_sem=recv_sem.at[which, k],
                device_id={"section": to},
                device_id_type=MESH,
            )
            copy.start()
            copies.append(copy)
    parts[me] = part_ref[me]
    mls[me] = ml_ref[me]
    for copy in copies:
        copy.wait()
    top = mls[0, 0:1, :]
    for i in range(1, n):
        top = jnp.maximum(top, mls[i, 0:1, :])
    total = jnp.zeros_like(top)
    for i in range(n):
        total = total + jnp.exp(mls[i, 0:1, :] - top) * mls[i, 1:2, :]
    coef[...] = jnp.zeros_like(coef)
    for i in range(n):
        coef[i : i + 1, :] = jnp.exp(mls[i, 0:1, :] - top) / total
    columns = coef[...].T
    result = jnp.zeros(out_ref.shape, jnp.float32)
    for i in range(n):
        result = result + parts[i].astype(jnp.float32) * columns[:, i : i + 1]
    out_ref[...] = result.astype(jnp.bfloat16)


def body(
    prompt_states,
    norm_gain,
    w_kv,
    pool_cache,
    queries,
    new_kv,
    ship_dest,
    page_row,
    finished,
    page_table,
    row_length,
):
    n = lax.axis_size("section")
    me = lax.axis_index("section")
    rows_dev, steps, width_q = queries.shape
    pool_pages, page_len, _, width_kv = pool_cache.shape
    kv_heads = width_kv // HS
    group = width_q // width_kv
    prompt_pages = prompt_states.shape[0] // page_len
    all_rows, max_pages = page_table.shape
    span = kv_heads * steps * group
    block = rows_dev * span

    own_q = queries.reshape(rows_dev, steps, kv_heads, group, HS).transpose(0, 2, 1, 3, 4)
    own_q = own_q.reshape(block, HS)
    all_q = pl.pallas_call(
        functools.partial(gather_kernel, n),
        out_shape=jax.ShapeDtypeStruct((n, block, HS), jnp.bfloat16),
        in_specs=[vmem()],
        out_specs=vmem(),
        scratch_shapes=[pltpu.SemaphoreType.DMA((n,)), pltpu.SemaphoreType.DMA((n,))],
        compiler_params=pltpu.CompilerParams(
            collective_id=0, has_side_effects=True, vmem_limit_bytes=VMEM_LIMIT
        ),
    )(own_q)

    states = prompt_states.astype(jnp.float32)
    spread = lax.rsqrt(jnp.mean(states * states, axis=-1, keepdims=True) + norm_epsilon)
    normed = (states * spread * norm_gain.astype(jnp.float32)).astype(jnp.bfloat16)
    prompt_kv = jnp.einsum("td,dkc->ktc", normed, w_kv, preferred_element_type=jnp.float32).astype(
        jnp.bfloat16
    )

    page_ids = me * pool_pages + jnp.arange(pool_pages, dtype=jnp.int32)
    page_hits = page_table[:, :, None] == page_ids[None, None, :]
    token_fill = jnp.clip(
        row_length[:, None] - jnp.arange(max_pages, dtype=jnp.int32)[None, :] * page_len,
        0,
        page_len,
    )
    row_ids = jnp.arange(all_rows, dtype=jnp.int32)
    packed = token_fill * all_rows + row_ids[:, None]
    found = jnp.sum(jnp.where(page_hits, packed[:, :, None], 0), axis=(0, 1))
    own_pages = me * prompt_pages
    dest = lax.dynamic_slice_in_dim(ship_dest[:, 0], own_pages, prompt_pages, 0)
    joined = lax.dynamic_slice_in_dim(page_row, own_pages, prompt_pages, 0)
    done = lax.dynamic_slice_in_dim(finished, own_pages, prompt_pages, 0)
    own_rows = me * rows_dev + jnp.arange(rows_dev, dtype=jnp.int32)
    rows = jnp.concatenate([found % all_rows, dest * rows_dev + joined, own_rows])
    counts = jnp.concatenate(
        [
            found // all_rows,
            jnp.where(done == 1, page_len, 0).astype(jnp.int32),
            jnp.zeros((rows_dev,), jnp.int32),
        ]
    )
    pool_k = pool_cache[:, :, 0].reshape(pool_pages * page_len, width_kv)
    pool_v = pool_cache[:, :, 1].reshape(pool_pages * page_len, width_kv)
    fresh = jnp.pad(new_kv, ((0, 0), (0, page_len - steps), (0, 0), (0, 0)))
    fresh_k = fresh[:, :, 0].reshape(rows_dev * page_len, width_kv)
    fresh_v = fresh[:, :, 1].reshape(rows_dev * page_len, width_kv)

    parts, mls = pl.pallas_call(
        functools.partial(attend_kernel, rows_dev, n),
        out_shape=(
            jax.ShapeDtypeStruct((n, block, HS), jnp.bfloat16),
            jax.ShapeDtypeStruct((n, 8, block), jnp.float32),
        ),
        in_specs=[smem(), smem()] + [vmem()] * 7,
        out_specs=(vmem(), vmem()),
        scratch_shapes=[pltpu.VMEM((n * block, HS), jnp.float32)] * 3,
        compiler_params=pltpu.CompilerParams(vmem_limit_bytes=VMEM_LIMIT),
    )(
        rows, counts, all_q.reshape(n * block, HS), pool_k, pool_v, prompt_kv[0], prompt_kv[1],
        fresh_k, fresh_v,
    )

    merged = pl.pallas_call(
        functools.partial(merge_kernel, n),
        out_shape=jax.ShapeDtypeStruct((block, HS), jnp.bfloat16),
        in_specs=[vmem(), vmem()],
        out_specs=vmem(),
        scratch_shapes=[
            pltpu.VMEM((n, block, HS), jnp.bfloat16),
            pltpu.VMEM((n, 8, block), jnp.float32),
            pltpu.VMEM((HS, block), jnp.float32),
            pltpu.SemaphoreType.DMA((2, n)),
            pltpu.SemaphoreType.DMA((2, n)),
        ],
        compiler_params=pltpu.CompilerParams(
            collective_id=1, has_side_effects=True, vmem_limit_bytes=VMEM_LIMIT
        ),
    )(parts, mls)
    heads = merged.reshape(rows_dev, kv_heads, steps, group, HS).transpose(0, 2, 1, 3, 4)
    return heads.reshape(rows_dev, steps, width_q)


def solution(mesh):
    return jax.shard_map(
        body,
        mesh=mesh,
        in_specs=(
            P(("groups", "section"), None),
            P(),
            P(None, None, "tensor"),
            P(("groups", "section"), None, None, "tensor"),
            P(("groups", "section"), None, "tensor"),
            P(("groups", "section"), None, None, "tensor"),
            P("groups", None),
            P("groups"),
            P("groups"),
            P("groups", None),
            P("groups"),
        ),
        out_specs=P(("groups", "section"), None, "tensor"),
        check_vma=False,
    )
```

time: 276 us -> 87.6 us (0.32)
  blocking collectives: 126 us -> 0 us
  Pallas kernels: 0 us -> 50.8 us
  waiting for transfers between devices: 40.2 us -> 0 us
  local copies, waits for them, and re-layouts: 40.1 us -> 14.1 us
  between operations: 14.5 us -> 0.18 us
  matrix products: 28.5 us -> 15 us
  other arithmetic: 17.3 us -> 6.48 us
  starting transfers between devices: 6.45 us -> 0 us
    all_gather x1 -> x0, blocking collectives: 56.2 us -> none  [body(): gathered_q = lax.all_gather(queries, 'section', axis=0, tiled=True)]
    pallas_call x0 -> x3, Pallas kernels: none -> 50.8 us  [the longest x1 18.6 us: body(): pl.pallas_call(functools.partial(attend_kernel, rows_dev, n), out_shape=(...]
    unnamed x2 -> x0, waiting for transfers between devices: 40.2 us -> none
    pmax x1 -> x0, blocking collectives: 36.1 us -> none  [body(): row_tops = lax.pmax(local_max, 'section')]
    unnamed x1 -> x0, blocking collectives: 33.8 us -> none
    dot_general x12 -> x1, matrix products: 28.5 us -> 15 us  [body(): jnp.einsum('td,dkc->ktc', normed, w_kv, preferred_element_type=jnp.float32)]
    slice x3 -> x2, local copies, waits for them, and re-layouts: 16.2 us -> 9.38 us  [the longest x1 9.36 us: body(): pool_v = pool_cache[:, :, 1].reshape(pool_pages * page_len, width_kv)]
    all_to_all x1 -> x0, starting transfers between devices: 6.41 us -> none  [body(): lax.all_to_all(outgoing, 'section', split_axis=0, concat_axis=0, tiled=True)]
  transfers between devices with their start and end apart: 2 -> 0, of which waited for: 1 -> 0; matrix products, arithmetic and copies ran while one was open for 14% -> 0% of each run, Pallas kernels for 0% -> 0%
where the time goes in v1:
time: 87.6 us; the launch traced here: 86.7 us
  Pallas kernels  50.8 us (58%)
  matrix products  15 us (17%)
  local copies, waits for them, and re-layouts  14.1 us (16%)
  other arithmetic  6.48 us (7%)
    pallas_call x1, Pallas kernels, body(): pl.pallas_call(functools.partial(attend_kernel, rows_dev, n), out_shape=(...  18.6 us
    pallas_call x1, Pallas kernels, body(): pl.pallas_call(functools.partial(merge_kernel, n), out_shape=jax.ShapeDty...  17.3 us
    dot_general x1, matrix products, body(): jnp.einsum('td,dkc->ktc', normed, w_kv, preferred_element_type=jnp.float32)  15 us
    pallas_call x1, Pallas kernels, body(): pl.pallas_call(functools.partial(gather_kernel, n), out_shape=jax.ShapeDt...  14.9 us
    slice x1, local copies, waits for them, and re-layouts, body(): pool_v = pool_cache[:, :, 1].reshape(pool_pages * page_len, width_kv)  9.36 us
    reduce_sum x1, other arithmetic, body(): jnp.mean(states * states, axis=-1, keepdims=True) + norm_epsilon  3.92 us
    unnamed x15, local copies, waits for them, and re-layouts  3 us

profile of v1, /device:TPU:8, one launch (start us, length us, event | category | flops | bytes accessed | tf_op | source)
XLA Modules:
  0.0 86.7 jit_solution(15239084451636465893)
XLA Ops:
  0.0 0.8 compare_select_fusion
  0.8 0.7 iota_add_fusion
  1.5 0.9 %select_reduce_fusion = s32[48]{0:T(128)S(1)} fusion(s32[32,12]{0,1:T(8,128)S(1)} %iota_add_fusion, s32[48]{0:T(128)S(1)} %iota_add_fusion.2, s32[32,12]{0,1:T(8,128)} %param.20), kind=kLoop, calls=%fused_computation.14 | loop fusion | flops 55248 | bytes 3456 | tf_op jit(solution)/shard_map/reduce_sum | solution.py:228
  2.4 0.1 pad_add_fusion.rows_ref
  2.5 0.1 pad_add_fusion.1.counts_ref
  2.6 0.0 copy-start.4
  2.6 0.0 copy-start.2
  2.6 9.4 %fusion.17 = (bf16[48,64,1,256]{3,2,1,0:T(2,128)(2,1)S(1)}, bf16[48,64,1,256]{3,2,1,0:T(2,128)(2,1)S(1)}) fusion(bf16[48,64,2,256]{3,2,1,0:T(2,128)(2,1)} %param.14), kind=kLoop, calls=%fused_computation.29 | loop fusion | bytes 6291456 | tf_op jit(solution)/shard_map/slice | solution.py:243
  11.9 0.4 copy.29
  12.4 0.4 copy.30
  12.9 0.0 copy-done.4
  12.9 0.0 copy-done.2
  12.9 3.9 %fusion = f32[1024]{0:T(1024)S(1)} fusion(bf16[1024,8192]{1,0:T(8,128)(2,1)S(1)} %copy-done.2), kind=kLoop, calls=%fused_computation.2 | loop fusion | flops 25164800 | bytes 16781312 | tf_op jit(solution)/shard_map/reduce_sum | solution.py:213
  16.8 0.0 copy-start.5
  16.8 0.0 copy-start.3
  16.8 15.0 %fusion.12 = bf16[2,1024,256]{2,1,0:T(8,128)(2,1)S(1)} fusion(bf16[8192,2,256]{2,1,0:T(2,128)(2,1)} %param.13, bf16[1024,8192]{1,0:T(8,128)(2,1)} %param.11, f32[8192]{0:T(1024)S(1)} %convert_element_type.18, f32[1024]{0:T(1024)S(1)} %add_rsqrt_fusion), kind=kOutput, calls=%fused_computation.9 | convolution fusion | flops 8624013312 | bytes 26251264 | tf_op jit(solution)/shard_map/td,dkc->ktc/dot_general | solution.py:215
  31.9 1.0 %slice_bitcast_fusion = (bf16[1024,256]{1,0:T(8,128)(2,1)}, bf16[1024,256]{1,0:T(8,128)(2,1)}) fusion(bf16[2,1024,256]{2,1,0:T(8,128)(2,1)S(1)} %fusion.12), kind=kLoop, calls=%fused_computation.10 | loop fusion | bytes 2097152 | tf_op jit(solution)/shard_map/squeeze | solution.py:259
  32.9 0.0 copy-done.5
  33.0 0.0 copy-done.3
  33.1 14.9 %shard_map.109 = bf16[8,256,128]{2,1,0:T(8,128)(2,1)S(1)} custom-call(bf16[256,128]{1,0:T(8,128)(2,1)S(1)} %bitcast.34), custom_call_target="tpu_custom_call" | custom-call | tf_op jit(solution)/shard_map/pallas_call | solution.py:201
  48.0 0.0 copy-start
  48.0 1.0 %copy-done = bf16[1024,256]{1,0:T(8,128)(2,1)S(1)} copy-done((bf16[1024,256]{1,0:T(8,128)(2,1)S(1)}, bf16[1024,256]{1,0:T(8,128)(2,1)}, u32[]{:S(2)}) %copy-start) | copy-done | bytes 524312
  49.1 0.0 copy-start.1
  49.1 1.0 %copy-done.1 = bf16[1024,256]{1,0:T(8,128)(2,1)S(1)} copy-done((bf16[1024,256]{1,0:T(8,128)(2,1)S(1)}, bf16[1024,256]{1,0:T(8,128)(2,1)}, u32[]{:S(2)}) %copy-start.1) | copy-done | bytes 524312
  50.1 18.6 %shard_map.110 = (bf16[8,256,128]{2,1,0:T(8,128)(2,1)S(1)}, f32[8,8,256]{2,1,0:T(8,128)S(1)}) custom-call(s32[68]{0:T(128)S(1)} %pad_add_fusion.rows_ref, s32[68]{0:T(128)S(1)} %pad_add_fusion.1.counts_ref, bf16[2048,128]{1,0:T(8,128)(2,1)S(1)} %bitcast.30, bf16[3072,256]{1,0:T(8,128)(2,1)S(1)} %bitcast.28, bf16[3072,256]{1,0:T(8,128)(2,1)S(1)} %bitcast.29, ...), custom_call_target="tpu_custom_call" | custom-call | tf_op jit(solution)/shard_map/pallas_call | solution.py:248
  68.7 17.3 %shard_map.111 = bf16[256,128]{1,0:T(8,128)(2,1)S(1)} custom-call(bf16[8,256,128]{2,1,0:T(8,128)(2,1)S(1)} %get-tuple-element.7.part_ref, f32[8,8,256]{2,1,0:T(8,128)S(1)} %get-tuple-element.8.ml_ref), custom_call_target="tpu_custom_call" | custom-call | tf_op jit(solution)/shard_map/pallas_call | solution.py:263
  86.0 0.6 reshape.78
  (12 shorter events, 0.1 us)
Async XLA Ops:
  2.6 10.3 %copy-start.4 = (bf16[8192]{0:T(1024)(128)(2,1)S(1)}, bf16[8192]{0:T(1024)(128)(2,1)}, u32[]{:S(2)}) copy-start(bf16[8192]{0:T(1024)(128)(2,1)} %param.12) | copy-start | bytes 49156
  2.6 10.3 %copy-start.2 = (bf16[1024,8192]{1,0:T(8,128)(2,1)S(1)}, bf16[1024,8192]{1,0:T(8,128)(2,1)}, u32[]{:S(2)}) copy-start(bf16[1024,8192]{1,0:T(8,128)(2,1)} %param.11) | copy-start | bytes 50331652
  16.8 16.1 %copy-start.5 = (bf16[4,4,2,256]{3,2,1,0:T(2,128)(2,1)S(1)}, bf16[4,4,2,256]{3,2,1,0:T(2,128)(2,1)}, u32[]{:S(2)}) copy-start(bf16[4,4,2,256]{3,2,1,0:T(2,128)(2,1)} %param.16) | copy-start | bytes 49156
  16.8 16.1 %copy-start.3 = (bf16[4,4,2048]{2,1,0:T(4,128)(2,1)S(1)}, bf16[4,4,2048]{2,1,0:T(4,128)(2,1)}, u32[]{:S(2)}) copy-start(bf16[4,4,2048]{2,1,0:T(4,128)(2,1)} %param.15) | copy-start | bytes 196612
  48.0 1.0 %copy-start = (bf16[1024,256]{1,0:T(8,128)(2,1)S(1)}, bf16[1024,256]{1,0:T(8,128)(2,1)}, u32[]{:S(2)}) copy-start(bf16[1024,256]{1,0:T(8,128)(2,1)} %get-tuple-element.11.prompt_v) | copy-start | bytes 1572868
  49.1 1.0 %copy-start.1 = (bf16[1024,256]{1,0:T(8,128)(2,1)S(1)}, bf16[1024,256]{1,0:T(8,128)(2,1)}, u32[]{:S(2)}) copy-start(bf16[1024,256]{1,0:T(8,128)(2,1)} %get-tuple-element.12.prompt_k) | copy-start | bytes 1572868

commit v2 on v1

--- a/solution.py
+++ b/solution.py
@@ -33,66 +33,64 @@
     pl.semaphore_wait(barrier, n - 1)
 
 
-def gather_kernel(n, own_ref, all_ref, send_sem, recv_sem):
-    me = lax.axis_index("section")
-    greet(n, me)
-    copies = []
-    for k in range(1, n):
-        copy = pltpu.make_async_remote_copy(
-            src_ref=own_ref,
-            dst_ref=all_ref.at[me],
-            send_sem=send_sem.at[k],
-            recv_sem=recv_sem.at[k],
-            device_id={"section": lax.rem(me + k, n)},
-            device_id_type=MESH,
-        )
-        copy.start()
-        copies.append(copy)
-    all_ref[me] = own_ref[...]
-    for copy in copies:
-        copy.wait()
-
-
 def attend_kernel(
-    rows_dev, n, rows_ref, counts_ref, q_ref, pool_k, pool_v, prompt_k, prompt_v, fresh_k, fresh_v,
-    out_ref, ml_ref, acc, tops, totals,
+    rows_dev, n, rows_ref, counts_ref, lookup_ref, pool, prompt_k, prompt_v, fresh, *rest
 ):
+    blocks = rest[:n]
+    out_ref, ml_ref, q_ref, acc, tops, totals = rest[n:]
+    for k in range(n):
+        size = blocks[k].shape[0]
+        q_ref[k * size : (k + 1) * size, :] = blocks[k][...]
     span = q_ref.shape[0] // (n * rows_dev)
     half = span // 2
     page_len = 64
-    pool_pages = pool_k.shape[0] // page_len
+    wide = 2 * page_len
+    pool_pages = pool.shape[0] // wide
     prompt_pages = prompt_k.shape[0] // page_len
     scale = 1.0 / math.sqrt(HS)
     acc[...] = jnp.zeros_like(acc)
     totals[...] = jnp.zeros_like(totals)
     tops[...] = jnp.full_like(tops, masked_value)
-    token = lax.broadcasted_iota(jnp.int32, (span, page_len), 1)
-    line = lax.broadcasted_iota(jnp.int32, (span, page_len), 0)
+    lane = lax.broadcasted_iota(jnp.int32, (span, wide), 1)
+    line = lax.broadcasted_iota(jnp.int32, (span, wide), 0)
     step = lax.rem(line, half) // 8
+    twice = jnp.where(lax.rem(lane, 2) == 0, lane // 2, page_len)
     contract_last = (((1,), (1,)), ((), ()))
 
-    def page_part(row, count, keys, values, at, causal):
-        q = q_ref[pl.ds(pl.multiple_of(row * span, span), span), :]
-        k = keys[pl.ds(pl.multiple_of(at * page_len, page_len), page_len), :]
-        v = values[pl.ds(pl.multiple_of(at * page_len, page_len), page_len), :]
+    def load_pair(ref, at):
+        return ref[pl.ds(pl.multiple_of(at * wide, wide), wide), :]
+
+    def load_split(refs, at):
+        here = pl.ds(pl.multiple_of(at * page_len, page_len), page_len)
+        return jnp.concatenate([refs[0][here, :], refs[1][here, :]], axis=0)
+
+    def page_part(place, count, pages, at, kind):
+        q = q_ref[pl.ds(pl.multiple_of(place * span, span), span), :]
+        kv = load_split(pages, at) if kind == "split" else load_pair(pages, at)
         low = lax.dot_general(
-            q[:half], k[:, :HS], contract_last, preferred_element_type=jnp.float32
+            q[:half], kv[:, :HS], contract_last, preferred_element_type=jnp.float32
         )
         high = lax.dot_general(
-            q[half:], k[:, HS:], contract_last, preferred_element_type=jnp.float32
+            q[half:], kv[:, HS:], contract_last, preferred_element_type=jnp.float32
         )
         scores = jnp.concatenate([low, high], axis=0) * scale
-        usable = (token <= step) if causal else (token < count)
+        if kind == "split":
+            usable = lane < count
+        elif kind == "fresh":
+            usable = twice <= step
+        else:
+            usable = twice < count
         scores = jnp.where(usable, scores, masked_value)
         top = jnp.max(scores, axis=1, keepdims=True)
         weights = jnp.where(usable, jnp.exp(scores - top), 0.0)
         total = jnp.sum(weights, axis=1, keepdims=True)
+        weights = pltpu.roll(weights, page_len if kind == "split" else 1, 1)
         main = weights.astype(jnp.bfloat16)
         rest = (weights - main.astype(jnp.float32)).astype(jnp.bfloat16)
         both_low = jnp.concatenate([main[:half], rest[:half]], axis=0)
         both_high = jnp.concatenate([main[half:], rest[half:]], axis=0)
-        sum_low = jnp.dot(both_low, v[:, :HS], preferred_element_type=jnp.float32)
-        sum_high = jnp.dot(both_high, v[:, HS:], preferred_element_type=jnp.float32)
+        sum_low = jnp.dot(both_low, kv[:, :HS], preferred_element_type=jnp.float32)
+        sum_high = jnp.dot(both_high, kv[:, HS:], preferred_element_type=jnp.float32)
         summed = jnp.concatenate(
             [sum_low[:half] + sum_low[half:], sum_high[:half] + sum_high[half:]], axis=0
         )
@@ -109,22 +107,23 @@
         totals[place, :] = totals[place, :] * keep + total * add
         acc[place, :] = acc[place, :] * keep + summed * add
 
-    def run(first, pages, keys, values, causal):
+    def run(first, count, pages, kind):
         def some(i, _):
             parts = []
             for u in range(UNROLL):
                 at = i * UNROLL + u
                 row = rows_ref[first + at]
-                parts.append((row, page_part(row, counts_ref[first + at], keys, values, at, causal)))
+                place = lookup_ref[first + at]
+                parts.append((row, page_part(place, counts_ref[first + at], pages, at, kind)))
             for row, part in parts:
                 update(row, part)
             return 0
 
-        lax.fori_loop(0, pages // UNROLL, some, 0)
-
-    run(0, pool_pages, pool_k, pool_v, False)
-    run(pool_pages, prompt_pages, prompt_k, prompt_v, False)
-    run(pool_pages + prompt_pages, rows_dev, fresh_k, fresh_v, True)
+        lax.fori_loop(0, count // UNROLL, some, 0)
+
+    run(0, pool_pages, pool, "pair")
+    run(pool_pages, prompt_pages, (prompt_k, prompt_v), "split")
+    run(pool_pages + prompt_pages, rows_dev, fresh, "fresh")
 
     block = rows_dev * span
     lane = lax.broadcasted_iota(jnp.int32, (block, HS), 1)
@@ -198,19 +197,16 @@
 
     own_q = queries.reshape(rows_dev, steps, kv_heads, group, HS).transpose(0, 2, 1, 3, 4)
     own_q = own_q.reshape(block, HS)
-    all_q = pl.pallas_call(
-        functools.partial(gather_kernel, n),
-        out_shape=jax.ShapeDtypeStruct((n, block, HS), jnp.bfloat16),
-        in_specs=[vmem()],
-        out_specs=vmem(),
-        scratch_shapes=[pltpu.SemaphoreType.DMA((n,)), pltpu.SemaphoreType.DMA((n,))],
-        compiler_params=pltpu.CompilerParams(
-            collective_id=0, has_side_effects=True, vmem_limit_bytes=VMEM_LIMIT
-        ),
-    )(own_q)
+    blocks = [own_q] + [
+        lax.ppermute(own_q, "section", [(i, (i + k) % n) for i in range(n)]) for k in range(1, n)
+    ]
 
     states = prompt_states.astype(jnp.float32)
     spread = lax.rsqrt(jnp.mean(states * states, axis=-1, keepdims=True) + norm_epsilon)
+    early = len(blocks) - 5
+    if early > 1:
+        spread, *first = lax.optimization_barrier((spread, *blocks[1:early]))
+        blocks[1:early] = first
     normed = (states * spread * norm_gain.astype(jnp.float32)).astype(jnp.bfloat16)
     prompt_kv = jnp.einsum("td,dkc->ktc", normed, w_kv, preferred_element_type=jnp.float32).astype(
         jnp.bfloat16
@@ -232,6 +228,7 @@
     done = lax.dynamic_slice_in_dim(finished, own_pages, prompt_pages, 0)
     own_rows = me * rows_dev + jnp.arange(rows_dev, dtype=jnp.int32)
     rows = jnp.concatenate([found % all_rows, dest * rows_dev + joined, own_rows])
+    lookup = (me + n - rows // rows_dev) % n * rows_dev + rows % rows_dev
     counts = jnp.concatenate(
         [
             found // all_rows,
@@ -239,11 +236,9 @@
             jnp.zeros((rows_dev,), jnp.int32),
         ]
     )
-    pool_k = pool_cache[:, :, 0].reshape(pool_pages * page_len, width_kv)
-    pool_v = pool_cache[:, :, 1].reshape(pool_pages * page_len, width_kv)
+    pool = pool_cache.reshape(pool_pages * page_len * 2, width_kv)
     fresh = jnp.pad(new_kv, ((0, 0), (0, page_len - steps), (0, 0), (0, 0)))
-    fresh_k = fresh[:, :, 0].reshape(rows_dev * page_len, width_kv)
-    fresh_v = fresh[:, :, 1].reshape(rows_dev * page_len, width_kv)
+    fresh = fresh.reshape(rows_dev * page_len * 2, width_kv)
 
     parts, mls = pl.pallas_call(
         functools.partial(attend_kernel, rows_dev, n),
@@ -251,13 +246,13 @@
             jax.ShapeDtypeStruct((n, block, HS), jnp.bfloat16),
             jax.ShapeDtypeStruct((n, 8, block), jnp.float32),
         ),
-        in_specs=[smem(), smem()] + [vmem()] * 7,
+        in_specs=[smem()] * 3 + [vmem()] * (4 + n),
         out_specs=(vmem(), vmem()),
-        scratch_shapes=[pltpu.VMEM((n * block, HS), jnp.float32)] * 3,
+        scratch_shapes=[pltpu.VMEM((n * block, HS), jnp.bfloat16)]
+        + [pltpu.VMEM((n * block, HS), jnp.float32)] * 3,
         compiler_params=pltpu.CompilerParams(vmem_limit_bytes=VMEM_LIMIT),
     )(
-        rows, counts, all_q.reshape(n * block, HS), pool_k, pool_v, prompt_kv[0], prompt_kv[1],
-        fresh_k, fresh_v,
+        rows, counts, lookup, pool, prompt_kv[0], prompt_kv[1], fresh, *blocks,
     )
 
     merged = pl.pallas_call(

time: 87.6 us -> 83.8 us (0.957)
  starting transfers between devices: 0 us -> 11.4 us
  Pallas kernels: 50.8 us -> 39.8 us
  local copies, waits for them, and re-layouts: 14.1 us -> 5.98 us
  other arithmetic: 6.48 us -> 11 us
    pallas_call x1 -> x0, Pallas kernels: 14.9 us -> none  [body(): pl.pallas_call(functools.partial(gather_kernel, n), out_shape=jax.ShapeDt...]
    ppermute x0 -> x7, starting transfers between devices: none -> 11.4 us  [body(): lax.ppermute(own_q, 'section', [(i, (i + k) % n) for i in range(n)])]
    slice x2 -> x0, local copies, waits for them, and re-layouts: 9.38 us -> none  [the longest x1 9.36 us: body(): pool_v = pool_cache[:, :, 1].reshape(pool_pages * page_len, width_kv)]
    pallas_call x1, Pallas kernels: 18.6 us -> 24.9 us  [body(): pl.pallas_call(functools.partial(attend_kernel, rows_dev, n), out_shape=(...]
    reshape x0 -> x2, local copies, waits for them, and re-layouts: none -> 4.13 us  [the longest x1 4.03 us: body(): pool = pool_cache.reshape(pool_pages * page_len * 2, width_kv)]
    reduce_sum x1, other arithmetic: 3.92 us -> 7.19 us  [body(): jnp.mean(states * states, axis=-1, keepdims=True) + norm_epsilon]
    unnamed x15 -> x12, local copies, waits for them, and re-layouts: 3 us -> 0.02 us
    pallas_call x1, Pallas kernels: 17.3 us -> 14.9 us  [body(): pl.pallas_call(functools.partial(merge_kernel, n), out_shape=jax.ShapeDty...]
  transfers between devices with their start and end apart: 0 -> 7, of which waited for: 0 -> 0; matrix products, arithmetic and copies ran while one was open for 0% -> 36% of each run, Pallas kernels for 0% -> 0%
where the time goes in v2:
time: 83.8 us; the launch traced here: 83.4 us
  Pallas kernels  39.8 us (47%)
  matrix products  15 us (18%)
  starting transfers between devices  11.4 us (14%)
  other arithmetic  11 us (13%)
  local copies, waits for them, and re-layouts  5.98 us (7%)
    pallas_call x1, Pallas kernels, body(): pl.pallas_call(functools.partial(attend_kernel, rows_dev, n), out_shape=(...  24.9 us
    dot_general x1, matrix products, body(): jnp.einsum('td,dkc->ktc', normed, w_kv, preferred_element_type=jnp.float32)  15 us
    pallas_call x1, Pallas kernels, body(): pl.pallas_call(functools.partial(merge_kernel, n), out_shape=jax.ShapeDty...  14.9 us
    ppermute x7, starting transfers between devices, body(): lax.ppermute(own_q, 'section', [(i, (i + k) % n) for i in range(n)])  11.4 us
    reduce_sum x1, other arithmetic, body(): jnp.mean(states * states, axis=-1, keepdims=True) + norm_epsilon  7.19 us
    reshape x1, local copies, waits for them, and re-layouts, body(): pool = pool_cache.reshape(pool_pages * page_len * 2, width_kv)  4.03 us
  transfers between devices with their start and end apart: 7, of which 0 were waited for; matrix products, arithmetic and copies ran while one was open for 36% of the time, Pallas kernels for 0%

profile of v2, /device:TPU:8, one launch (start us, length us, event | category | flops | bytes accessed | tf_op | source)
XLA Modules:
  0.0 83.4 jit_solution(14208944180835547655)
XLA Ops:
  0.0 0.9 %reshape.91 = bf16[4,4,2,8,128]{4,3,2,1,0:T(8,128)(2,1)S(1)} reshape(bf16[4,4,2048]{2,1,0:T(4,128)(2,1)} %param.15) | data formatting | bytes 131072 | tf_op jit(solution)/shard_map/reshape | solution.py:198
  1.0 1.5 %collective-permute-start.6 = (bf16[256,128]{1,0:T(8,128)(2,1)S(1)}, bf16[256,128]{1,0:T(8,128)(2,1)S(1)}, u32[]{:S(2)}, u32[]{:S(2)}) collective-permute-start(bf16[256,128]{1,0:T(8,128)(2,1)S(1)} %bitcast.25), channel_id=1, source_target_pairs={{0,14},{2,0},{4,2},{6,4},{8,6},{10,8},{12,10},{14,12},{1,15},{3,1}... | collective-permute-start | bytes 196616 | tf_op jit(solution)/shard_map/ppermute | solution.py:201
  2.5 3.6 %collective-permute-start.5 = (bf16[256,128]{1,0:T(8,128)(2,1)S(1)}, bf16[256,128]{1,0:T(8,128)(2,1)}, u32[]{:S(2)}, u32[]{:S(2)}) collective-permute-start(bf16[256,128]{1,0:T(8,128)(2,1)S(1)} %bitcast.26), channel_id=1, source_target_pairs={{0,12},{2,14},{4,0},{6,2},{8,4},{10,6},{12,8},{14,10},{1,13},{3,15... | collective-permute-start | bytes 196616 | tf_op jit(solution)/shard_map/ppermute | solution.py:201
  6.1 0.0 collective-permute-start.4
  6.1 2.0 %collective-permute-start.1 = (bf16[256,128]{1,0:T(8,128)(2,1)S(1)}, bf16[256,128]{1,0:T(8,128)(2,1)}, u32[]{:S(2)}, u32[]{:S(2)}) collective-permute-start(bf16[256,128]{1,0:T(8,128)(2,1)S(1)} %bitcast.28), channel_id=1, source_target_pairs={{0,4},{2,6},{4,8},{6,10},{8,12},{10,14},{12,0},{14,2},{1,5},{3,7},... | collective-permute-start | bytes 196616 | tf_op jit(solution)/shard_map/ppermute | solution.py:201
  8.0 1.5 %collective-permute-start = (bf16[256,128]{1,0:T(8,128)(2,1)S(1)}, bf16[256,128]{1,0:T(8,128)(2,1)}, u32[]{:S(2)}, u32[]{:S(2)}) collective-permute-start(bf16[256,128]{1,0:T(8,128)(2,1)S(1)} %bitcast.29), channel_id=1, source_target_pairs={{0,2},{2,4},{4,6},{6,8},{8,10},{10,12},{12,14},{14,0},{1,3},{3,5},... | collective-permute-start | bytes 196616 | tf_op jit(solution)/shard_map/ppermute | solution.py:201
  9.6 7.2 %fusion = f32[1024]{0:T(1024)S(1)} fusion(bf16[1024,8192]{1,0:T(8,128)(2,1)} %param.11), kind=kLoop, calls=%fused_computation.2 | loop fusion | flops 25164800 | bytes 16781312 | tf_op jit(solution)/shard_map/reduce_sum | solution.py:205
  16.8 0.1 iota_add_fusion
  16.9 0.2 select_reduce_fusion
  17.0 0.6 and_select_fusion.3
  17.7 0.6 convert_element_type.18
  18.3 0.1 pad.4
  18.4 0.1 reshape.93.fresh
  18.5 4.0 %reshape.90.pool = bf16[6144,256]{1,0:T(8,128)(2,1)S(1)} reshape(bf16[48,64,2,256]{3,2,1,0:T(2,128)(2,1)} %param.14) | data formatting | bytes 6291456 | tf_op jit(solution)/shard_map/reshape | solution.py:239
  22.6 0.7 compare_select_fusion.2
  23.3 0.1 bitcast_add_fusion
  23.4 0.8 fusion.17
  24.2 0.7 pad_add_fusion.1.counts_ref
  24.9 0.0 collective-permute-done.1.rest_2_
  24.9 1.2 %collective-permute-start.3 = (bf16[256,128]{1,0:T(8,128)(2,1)S(1)}, bf16[256,128]{1,0:T(8,128)(2,1)S(1)}, u32[]{:S(2)}, u32[]{:S(2)}) collective-permute-start(bf16[256,128]{1,0:T(8,128)(2,1)S(1)} %bitcast.30), channel_id=1, source_target_pairs={{0,8},{2,10},{4,12},{6,14},{8,0},{10,2},{12,4},{14,6},{1,9},{3,11}... | collective-permute-start | bytes 196616 | tf_op jit(solution)/shard_map/ppermute | solution.py:201
  26.2 0.0 collective-permute-done.rest_1_
  26.2 1.6 %collective-permute-start.2 = (bf16[256,128]{1,0:T(8,128)(2,1)S(1)}, bf16[256,128]{1,0:T(8,128)(2,1)S(1)}, u32[]{:S(2)}, u32[]{:S(2)}) collective-permute-start(bf16[256,128]{1,0:T(8,128)(2,1)S(1)} %bitcast.31), channel_id=1, source_target_pairs={{0,6},{2,8},{4,10},{6,12},{8,14},{10,0},{12,2},{14,4},{1,7},{3,9},... | collective-permute-start | bytes 196616 | tf_op jit(solution)/shard_map/ppermute | solution.py:201
  27.8 15.0 %fusion.12 = bf16[2,1024,256]{2,1,0:T(8,128)(2,1)S(1)} fusion(bf16[8192,2,256]{2,1,0:T(2,128)(2,1)} %param.13, bf16[1024,8192]{1,0:T(8,128)(2,1)} %param.11, f32[8192]{0:T(1024)} %convert_element_type.18, f32[1024]{0:T(1024)S(1)} %add_rsqrt_fusion), kind=kOutput, calls=%fused_computation.9 | convolution fusion | flops 8624013312 | bytes 26251264 | tf_op jit(solution)/shard_map/td,dkc->ktc/dot_general | solution.py:211
  42.8 0.1 slice_bitcast_fusion
  42.9 0.0 collective-permute-done.6.rest_7_
  42.9 0.0 collective-permute-done.5.rest_6_
  42.9 0.0 collective-permute-done.4.rest_5_
  42.9 0.0 collective-permute-done.3.rest_4_
  42.9 0.0 collective-permute-done.2.rest_3_
  42.9 24.9 %shard_map.109 = (bf16[8,256,128]{2,1,0:T(8,128)(2,1)S(1)}, f32[8,8,256]{2,1,0:T(8,128)S(1)}) custom-call(s32[68]{0:T(128)S(1)} %get-tuple-element.16.rows_ref, s32[68]{0:T(128)S(1)} %pad_add_fusion.1.counts_ref, s32[68]{0:T(128)S(1)} %get-tuple-element.15.lookup_ref, bf16[6144,256]{1,0:T(8,128)(2,1)S(1)} %reshape.90.pool, ...), custom_call_target="tpu_custom_call" | custom-call | tf_op jit(solution)/shard_map/pallas_call | solution.py:243
  67.9 14.9 %shard_map.110 = bf16[256,128]{1,0:T(8,128)(2,1)S(1)} custom-call(bf16[8,256,128]{2,1,0:T(8,128)(2,1)S(1)} %get-tuple-element.13.part_ref, f32[8,8,256]{2,1,0:T(8,128)S(1)} %get-tuple-element.14.ml_ref), custom_call_target="tpu_custom_call" | custom-call | tf_op jit(solution)/shard_map/pallas_call | solution.py:258
  82.8 0.6 reshape.95
  (19 shorter events, 0.1 us)
Async XLA Ops:
  0.0 16.8 %copy-start.3 = (s32[32]{0:T(128)S(1)}, s32[32]{0:T(128)}, u32[]{:S(2)}) copy-start(s32[32]{0:T(128)} %param.21) | copy-start | bytes 388
  0.0 16.9 %copy-start.2 = (s32[32,12]{0,1:T(8,128)S(1)}, s32[32,12]{0,1:T(8,128)}, u32[]{:S(2)}) copy-start(s32[32,12]{0,1:T(8,128)} %param.20) | copy-start | bytes 4612
  0.0 17.7 %copy-start = (bf16[8192]{0:T(1024)(128)(2,1)S(1)}, bf16[8192]{0:T(1024)(128)(2,1)}, u32[]{:S(2)}) copy-start(bf16[8192]{0:T(1024)(128)(2,1)} %param.12) | copy-start | bytes 49156
  0.0 18.3 %copy-start.1 = (bf16[4,4,2,256]{3,2,1,0:T(2,128)(2,1)S(1)}, bf16[4,4,2,256]{3,2,1,0:T(2,128)(2,1)}, u32[]{:S(2)}) copy-start(bf16[4,4,2,256]{3,2,1,0:T(2,128)(2,1)} %param.16) | copy-start | bytes 49156
  0.0 23.3 %copy-start.4 = (s32[128]{0:T(128)S(1)}, s32[128]{0:T(128)}, u32[]{:S(2)}) copy-start(s32[128]{0:T(128)} %param.18) | copy-start | bytes 1540
  0.0 23.3 %copy-start.5 = (s32[128,1]{0,1:T(1,128)S(1)}, s32[128,1]{0,1:T(1,128)}, u32[]{:S(2)}) copy-start(s32[128,1]{0,1:T(1,128)} %param.17) | copy-start | bytes 1540
  1.0 41.9 %collective-permute-start.6 = (bf16[256,128]{1,0:T(8,128)(2,1)S(1)}, bf16[256,128]{1,0:T(8,128)(2,1)S(1)}, u32[]{:S(2)}, u32[]{:S(2)}) collective-permute-start(bf16[256,128]{1,0:T(8,128)(2,1)S(1)} %bitcast.25), channel_id=1, source_target_pairs={{0,14},{2,0},{4,2},{6,4},{8,6},{10,8},{12,10},{14,12},{1,15},{3,1}... | collective-permute-start | bytes 196616 | tf_op jit(solution)/shard_map/ppermute | solution.py:201
  2.5 40.4 %collective-permute-start.5 = (bf16[256,128]{1,0:T(8,128)(2,1)S(1)}, bf16[256,128]{1,0:T(8,128)(2,1)}, u32[]{:S(2)}, u32[]{:S(2)}) collective-permute-start(bf16[256,128]{1,0:T(8,128)(2,1)S(1)} %bitcast.26), channel_id=1, source_target_pairs={{0,12},{2,14},{4,0},{6,2},{8,4},{10,6},{12,8},{14,10},{1,13},{3,15... | collective-permute-start | bytes 196616 | tf_op jit(solution)/shard_map/ppermute | solution.py:201
  6.1 36.9 %collective-permute-start.4 = (bf16[256,128]{1,0:T(8,128)(2,1)S(1)}, bf16[256,128]{1,0:T(8,128)(2,1)}, u32[]{:S(2)}, u32[]{:S(2)}) collective-permute-start(bf16[256,128]{1,0:T(8,128)(2,1)S(1)} %bitcast.27), channel_id=1, source_target_pairs={{0,10},{2,12},{4,14},{6,0},{8,2},{10,4},{12,6},{14,8},{1,11},{3,13... | collective-permute-start | bytes 196616 | tf_op jit(solution)/shard_map/ppermute | solution.py:201
  6.1 18.9 %collective-permute-start.1 = (bf16[256,128]{1,0:T(8,128)(2,1)S(1)}, bf16[256,128]{1,0:T(8,128)(2,1)}, u32[]{:S(2)}, u32[]{:S(2)}) collective-permute-start(bf16[256,128]{1,0:T(8,128)(2,1)S(1)} %bitcast.28), channel_id=1, source_target_pairs={{0,4},{2,6},{4,8},{6,10},{8,12},{10,14},{12,0},{14,2},{1,5},{3,7},... | collective-permute-start | bytes 196616 | tf_op jit(solution)/shard_map/ppermute | solution.py:201
  8.0 18.1 %collective-permute-start = (bf16[256,128]{1,0:T(8,128)(2,1)S(1)}, bf16[256,128]{1,0:T(8,128)(2,1)}, u32[]{:S(2)}, u32[]{:S(2)}) collective-permute-start(bf16[256,128]{1,0:T(8,128)(2,1)S(1)} %bitcast.29), channel_id=1, source_target_pairs={{0,2},{2,4},{4,6},{6,8},{8,10},{10,12},{12,14},{14,0},{1,3},{3,5},... | collective-permute-start | bytes 196616 | tf_op jit(solution)/shard_map/ppermute | solution.py:201
  24.9 18.0 %collective-permute-start.3 = (bf16[256,128]{1,0:T(8,128)(2,1)S(1)}, bf16[256,128]{1,0:T(8,128)(2,1)S(1)}, u32[]{:S(2)}, u32[]{:S(2)}) collective-permute-start(bf16[256,128]{1,0:T(8,128)(2,1)S(1)} %bitcast.30), channel_id=1, source_target_pairs={{0,8},{2,10},{4,12},{6,14},{8,0},{10,2},{12,4},{14,6},{1,9},{3,11}... | collective-permute-start | bytes 196616 | tf_op jit(solution)/shard_map/ppermute | solution.py:201
  26.2 16.8 %collective-permute-start.2 = (bf16[256,128]{1,0:T(8,128)(2,1)S(1)}, bf16[256,128]{1,0:T(8,128)(2,1)S(1)}, u32[]{:S(2)}, u32[]{:S(2)}) collective-permute-start(bf16[256,128]{1,0:T(8,128)(2,1)S(1)} %bitcast.31), channel_id=1, source_target_pairs={{0,6},{2,8},{4,10},{6,12},{8,14},{10,0},{12,2},{14,4},{1,7},{3,9},... | collective-permute-start | bytes 196616 | tf_op jit(solution)/shard_map/ppermute | solution.py:201

commit v3 on v2

--- a/solution.py
+++ b/solution.py
@@ -13,7 +13,7 @@
 masked_value = -1e30
 norm_epsilon = 1e-05
 VMEM_LIMIT = 48 * 1024 * 1024
-UNROLL = 4
+UNROLL = 8
 
 
 def vmem():
@@ -34,15 +34,21 @@
 
 
 def attend_kernel(
-    rows_dev, n, rows_ref, counts_ref, lookup_ref, pool, prompt_k, prompt_v, fresh, *rest
+    rows_dev, n, pieces, rows_ref, counts_ref, lookup_ref, pool, prompt_k, prompt_v, fresh, *others
 ):
-    blocks = rest[:n]
-    out_ref, ml_ref, q_ref, acc, tops, totals = rest[n:]
-    for k in range(n):
-        size = blocks[k].shape[0]
-        q_ref[k * size : (k + 1) * size, :] = blocks[k][...]
+    blocks = others[:pieces]
+    out_ref, ml_ref, q_ref, acc, tops, totals = others[pieces:]
     span = q_ref.shape[0] // (n * rows_dev)
     half = span // 2
+    start = 0
+    for piece in blocks:
+        size = piece.shape[0]
+        q = piece[...]
+        of_low = lax.rem(lax.broadcasted_iota(jnp.int32, q.shape, 0), span) < half
+        zero = jnp.zeros_like(q)
+        q_ref[start : start + size, :HS] = jnp.where(of_low, q, zero)
+        q_ref[start : start + size, HS:] = jnp.where(of_low, zero, q)
+        start += size
     page_len = 64
     wide = 2 * page_len
     pool_pages = pool.shape[0] // wide
@@ -67,13 +73,9 @@
     def page_part(place, count, pages, at, kind):
         q = q_ref[pl.ds(pl.multiple_of(place * span, span), span), :]
         kv = load_split(pages, at) if kind == "split" else load_pair(pages, at)
-        low = lax.dot_general(
-            q[:half], kv[:, :HS], contract_last, preferred_element_type=jnp.float32
-        )
-        high = lax.dot_general(
-            q[half:], kv[:, HS:], contract_last, preferred_element_type=jnp.float32
-        )
-        scores = jnp.concatenate([low, high], axis=0) * scale
+        scores = lax.dot_general(
+            q, kv, contract_last, preferred_element_type=jnp.float32
+        ) * scale
         if kind == "split":
             usable = lane < count
         elif kind == "fresh":
@@ -108,10 +110,12 @@
         acc[place, :] = acc[place, :] * keep + summed * add
 
     def run(first, count, pages, kind):
+        many = math.gcd(count, UNROLL)
+
         def some(i, _):
             parts = []
-            for u in range(UNROLL):
-                at = i * UNROLL + u
+            for u in range(many):
+                at = i * many + u
                 row = rows_ref[first + at]
                 place = lookup_ref[first + at]
                 parts.append((row, page_part(place, counts_ref[first + at], pages, at, kind)))
@@ -119,7 +123,7 @@
                 update(row, part)
             return 0
 
-        lax.fori_loop(0, count // UNROLL, some, 0)
+        lax.fori_loop(0, count // many, some, 0)
 
     run(0, pool_pages, pool, "pair")
     run(pool_pages, prompt_pages, (prompt_k, prompt_v), "split")
@@ -171,6 +175,11 @@
     out_ref[...] = result.astype(jnp.bfloat16)
 
 
+def row_spread(prompts):
+    states = prompts.astype(jnp.float32)
+    return lax.rsqrt(jnp.mean(states * states, axis=-1, keepdims=True) + norm_epsilon)
+
+
 def body(
     prompt_states,
     norm_gain,
@@ -197,16 +206,26 @@
 
     own_q = queries.reshape(rows_dev, steps, kv_heads, group, HS).transpose(0, 2, 1, 3, 4)
     own_q = own_q.reshape(block, HS)
-    blocks = [own_q] + [
-        lax.ppermute(own_q, "section", [(i, (i + k) % n) for i in range(n)]) for k in range(1, n)
-    ]
-
-    states = prompt_states.astype(jnp.float32)
-    spread = lax.rsqrt(jnp.mean(states * states, axis=-1, keepdims=True) + norm_epsilon)
-    early = len(blocks) - 5
-    if early > 1:
-        spread, *first = lax.optimization_barrier((spread, *blocks[1:early]))
-        blocks[1:early] = first
+    blocks = [own_q]
+    pool = pool_cache.reshape(pool_pages * page_len * 2, width_kv)
+    prompts = prompt_states
+    spread = None
+    size = 1
+    while size < n:
+        whole = blocks[0] if size == 1 else jnp.concatenate(blocks, axis=0)
+        other = lax.ppermute(whole, "section", [(i, i ^ size) for i in range(n)])
+        if 2 * size == n:
+            pass
+        elif size == 1:
+            other, pool, prompts = lax.optimization_barrier((other, pool, prompts))
+        elif 4 * size == n:
+            spread = row_spread(prompts)
+            other, spread = lax.optimization_barrier((other, spread))
+        blocks.append(other)
+        size *= 2
+    if spread is None:
+        spread = row_spread(prompts)
+    states = prompts.astype(jnp.float32)
     normed = (states * spread * norm_gain.astype(jnp.float32)).astype(jnp.bfloat16)
     prompt_kv = jnp.einsum("td,dkc->ktc", normed, w_kv, preferred_element_type=jnp.float32).astype(
         jnp.bfloat16
@@ -228,7 +247,7 @@
     done = lax.dynamic_slice_in_dim(finished, own_pages, prompt_pages, 0)
     own_rows = me * rows_dev + jnp.arange(rows_dev, dtype=jnp.int32)
     rows = jnp.concatenate([found % all_rows, dest * rows_dev + joined, own_rows])
-    lookup = (me + n - rows // rows_dev) % n * rows_dev + rows % rows_dev
+    lookup = (me ^ (rows // rows_dev)) * rows_dev + rows % rows_dev
     counts = jnp.concatenate(
         [
             found // all_rows,
@@ -236,19 +255,18 @@
             jnp.zeros((rows_dev,), jnp.int32),
         ]
     )
-    pool = pool_cache.reshape(pool_pages * page_len * 2, width_kv)
     fresh = jnp.pad(new_kv, ((0, 0), (0, page_len - steps), (0, 0), (0, 0)))
     fresh = fresh.reshape(rows_dev * page_len * 2, width_kv)
 
     parts, mls = pl.pallas_call(
-        functools.partial(attend_kernel, rows_dev, n),
+        functools.partial(attend_kernel, rows_dev, n, len(blocks)),
         out_shape=(
             jax.ShapeDtypeStruct((n, block, HS), jnp.bfloat16),
             jax.ShapeDtypeStruct((n, 8, block), jnp.float32),
         ),
-        in_specs=[smem()] * 3 + [vmem()] * (4 + n),
+        in_specs=[smem()] * 3 + [vmem()] * (4 + len(blocks)),
         out_specs=(vmem(), vmem()),
-        scratch_shapes=[pltpu.VMEM((n * block, HS), jnp.bfloat16)]
+        scratch_shapes=[pltpu.VMEM((n * block, 2 * HS), jnp.bfloat16)]
         + [pltpu.VMEM((n * block, HS), jnp.float32)] * 3,
         compiler_params=pltpu.CompilerParams(vmem_limit_bytes=VMEM_LIMIT),
     )(

time: 83.8 us -> 65.4 us (0.78)
  Pallas kernels: 39.8 us -> 24.9 us
  starting transfers between devices: 11.4 us -> 4.75 us
  local copies, waits for them, and re-layouts: 5.98 us -> 8.26 us
    pallas_call x1, Pallas kernels: 24.9 us -> 8.69 us  [body(): pl.pallas_call(functools.partial(attend_kernel, rows_dev, n, len(blocks))...]
    ppermute x7 -> x3, starting transfers between devices: 11.4 us -> 4.75 us  [body(): other = lax.ppermute(whole, 'section', [(i, i ^ size) for i in range(n)])]
    pad x1, local copies, waits for them, and re-layouts: 0.14 us -> 1.54 us  [body(): fresh = jnp.pad(new_kv, ((0, 0), (0, page_len - steps), (0, 0), (0, 0)))]
    pallas_call x1, Pallas kernels: 14.9 us -> 16.2 us  [body(): pl.pallas_call(functools.partial(merge_kernel, n), out_shape=jax.ShapeDty...]
    reshape x1, local copies, waits for them, and re-layouts: 0.1 us -> 1.05 us  [body(): fresh = fresh.reshape(rows_dev * page_len * 2, width_kv)]
  transfers between devices with their start and end apart: 7 -> 3, of which waited for: 0 -> 0; matrix products, arithmetic and copies ran while one was open for 36% -> 52% of each run, Pallas kernels for 0% -> 0%
where the time goes in v3:
time: 65.4 us; the launch traced here: 64.9 us
  Pallas kernels  24.9 us (38%)
  matrix products  15 us (23%)
  other arithmetic  11.8 us (18%)
  local copies, waits for them, and re-layouts  8.26 us (13%)
  starting transfers between devices  4.75 us (7%)
    pallas_call x1, Pallas kernels, body(): pl.pallas_call(functools.partial(merge_kernel, n), out_shape=jax.ShapeDty...  16.2 us
    dot_general x1, matrix products, body(): jnp.einsum('td,dkc->ktc', normed, w_kv, preferred_element_type=jnp.float32)  15 us
    pallas_call x1, Pallas kernels, body(): pl.pallas_call(functools.partial(attend_kernel, rows_dev, n, len(blocks))...  8.69 us
    reduce_sum x1, other arithmetic, row_spread(): jnp.mean(states * states, axis=-1, keepdims=True) + norm_epsilon  7.18 us
    ppermute x3, starting transfers between devices, body(): other = lax.ppermute(whole, 'section', [(i, i ^ size) for i in range(n)])  4.75 us
    reshape x1, local copies, waits for them, and re-layouts, body(): pool = pool_cache.reshape(pool_pages * page_len * 2, width_kv)  4.03 us
    pad x1, local copies, waits for them, and re-layouts, body(): fresh = jnp.pad(new_kv, ((0, 0), (0, page_len - steps), (0, 0), (0, 0)))  1.54 us
    convert_element_type x1, other arithmetic, body(): norm_gain.astype(jnp.float32)  1.34 us
  transfers between devices with their start and end apart: 3, of which 0 were waited for; matrix products, arithmetic and copies ran while one was open for 52% of the time, Pallas kernels for 0%

profile of v3, /device:TPU:8, one launch (start us, length us, event | category | flops | bytes accessed | tf_op | source)
XLA Modules:
  0.0 64.9 jit_solution(4916341505361331418)
XLA Ops:
  0.0 0.9 %reshape.90 = bf16[4,4,2,8,128]{4,3,2,1,0:T(8,128)(2,1)S(1)} reshape(bf16[4,4,2048]{2,1,0:T(4,128)(2,1)} %param.15) | data formatting | bytes 131072 | tf_op jit(solution)/shard_map/reshape | solution.py:207
  0.9 1.6 %collective-permute-start = (bf16[256,128]{1,0:T(8,128)(2,1)S(1)}, bf16[256,128]{1,0:T(8,128)(2,1)S(1)}, u32[]{:S(2)}, u32[]{:S(2)}) collective-permute-start(bf16[256,128]{1,0:T(8,128)(2,1)S(1)} %bitcast.25), channel_id=1, source_target_pairs={{0,2},{2,0},{4,6},{6,4},{8,10},{10,8},{12,14},{14,12},{1,3},{3,1},... | collective-permute-start | bytes 196616 | tf_op jit(solution)/shard_map/ppermute | solution.py:216
  2.5 0.7 %iota_add_fusion = s32[32,12]{0,1:T(8,128)S(1)} fusion(s32[12]{0:T(128)S(1)} %iota_multiply_fusion, s32[32]{0:T(128)} %param.21), kind=kLoop, calls=%fused_computation.15 | loop fusion | flops 1536 | bytes 1712 | tf_op jit(solution)/shard_map/add | solution.py:242
  3.2 0.9 %select_reduce_fusion = s32[48]{0:T(128)S(1)} fusion(s32[32,12]{0,1:T(8,128)S(1)} %iota_add_fusion, s32[48]{0:T(128)S(1)} %iota_add_fusion.2, s32[32,12]{0,1:T(8,128)} %param.20), kind=kLoop, calls=%fused_computation.13 | loop fusion | flops 55248 | bytes 3456 | tf_op jit(solution)/shard_map/reduce_sum | solution.py:243
  4.1 4.0 %reshape.92.pool = bf16[6144,256]{1,0:T(8,128)(2,1)S(1)} reshape(bf16[48,64,2,256]{3,2,1,0:T(2,128)(2,1)} %param.14) | data formatting | bytes 6291456 | tf_op jit(solution)/shard_map/reshape | solution.py:210
  8.2 1.3 %convert_element_type.19 = f32[8192]{0:T(1024)} convert(bf16[8192]{0:T(1024)(128)(2,1)} %param.12) | non-fusion elementwise | flops 8192 | bytes 49152 | tf_op jit(solution)/shard_map/convert_element_type | solution.py:229
  9.5 1.5 %pad.4 = bf16[4,64,2,256]{3,2,1,0:T(2,128)(2,1)} pad(bf16[4,4,2,256]{3,2,1,0:T(2,128)(2,1)} %param.16, bf16[]{:T(256)} %constant.83.clone.1), padding=0_0x0_60x0_0x0_0 | pad | bytes 278530 | tf_op jit(solution)/shard_map/jit(_pad)/pad | solution.py:258
  11.0 1.1 %reshape.93.fresh = bf16[512,256]{1,0:T(8,128)(2,1)S(1)} reshape(bf16[4,64,2,256]{3,2,1,0:T(2,128)(2,1)} %pad.4) | data formatting | bytes 524288 | tf_op jit(solution)/shard_map/reshape | solution.py:259
  12.1 0.0 copy-start
  12.1 0.7 %compare_select_fusion = s32[16]{0:T(128)S(1)} fusion(s32[128]{0:T(128)} %param.19, s32[]{:T(128)S(6)} %select_n.38), kind=kLoop, calls=%fused_computation.19 | loop fusion | flops 32 | bytes 132 | tf_op jit(solution)/shard_map/jit(_where)/select_n | solution.py:254
  12.8 0.7 %bitcast_add_fusion = s32[16]{0:T(128)S(1)} fusion(s32[128]{0:T(128)} %param.18, s32[]{:T(128)S(6)} %select_n.38, s32[128,1]{0,1:T(1,128)} %param.17), kind=kLoop, calls=%fused_computation.31 | loop fusion | flops 32 | bytes 196 | tf_op jit(solution)/shard_map/add | solution.py:249
  13.6 0.1 fusion.17
  13.7 0.1 pad_add_fusion.1.counts_ref
  13.8 0.0 collective-permute-done.others_1_
  13.8 0.5 collective-permute-start.1
  14.3 7.2 %fusion = f32[1024]{0:T(1024)S(1)} fusion(bf16[1024,8192]{1,0:T(8,128)(2,1)} %param.11), kind=kLoop, calls=%fused_computation.2 | loop fusion | flops 25164800 | bytes 16781312 | tf_op jit(solution)/shard_map/reduce_sum | solution.py:180
  21.5 0.0 collective-permute-done.1.others_2_
  21.5 2.7 %collective-permute-start.2 = (bf16[1024,128]{1,0:T(8,128)(2,1)S(1)}, bf16[1024,128]{1,0:T(8,128)(2,1)S(1)}, u32[]{:S(2)}, u32[]{:S(2)}) collective-permute-start(bf16[1024,128]{1,0:T(8,128)(2,1)S(1)} %pad_maximum_fusion), channel_id=1, source_target_pairs={{0,8},{2,10},{4,12},{6,14},{8,0},{10,2},{12,4},{14,6},{1,9},{3,11}... | collective-permute-start | bytes 786440 | tf_op jit(solution)/shard_map/ppermute | solution.py:216
  24.2 0.0 copy-done
  24.2 15.0 %fusion.12 = bf16[2,1024,256]{2,1,0:T(8,128)(2,1)S(1)} fusion(bf16[8192,2,256]{2,1,0:T(2,128)(2,1)} %param.13, bf16[1024,8192]{1,0:T(8,128)(2,1)} %param.11, f32[8192]{0:T(1024)S(1)} %copy-done, f32[1024]{0:T(1024)S(1)} %add_rsqrt_fusion), kind=kOutput, calls=%fused_computation.9 | convolution fusion | flops 8624013312 | bytes 26251264 | tf_op jit(solution)/shard_map/td,dkc->ktc/dot_general | solution.py:230
  39.2 0.1 slice_bitcast_fusion
  39.3 0.0 collective-permute-done.2.others_3_
  39.3 8.7 %shard_map.109 = (bf16[8,256,128]{2,1,0:T(8,128)(2,1)S(1)}, f32[8,8,256]{2,1,0:T(8,128)S(1)}) custom-call(s32[68]{0:T(128)S(1)} %get-tuple-element.20.rows_ref, s32[68]{0:T(128)S(1)} %pad_add_fusion.1.counts_ref, s32[68]{0:T(128)S(1)} %get-tuple-element.19.lookup_ref, bf16[6144,256]{1,0:T(8,128)(2,1)S(1)} %reshape.92.pool, ...), custom_call_target="tpu_custom_call" | custom-call | tf_op jit(solution)/shard_map/pallas_call | solution.py:261
  48.0 16.2 %shard_map.110 = bf16[256,128]{1,0:T(8,128)(2,1)S(1)} custom-call(bf16[8,256,128]{2,1,0:T(8,128)(2,1)S(1)} %get-tuple-element.17.part_ref, f32[8,8,256]{2,1,0:T(8,128)S(1)} %get-tuple-element.18.ml_ref), custom_call_target="tpu_custom_call" | custom-call | tf_op jit(solution)/shard_map/pallas_call | solution.py:276
  64.3 0.6 %reshape.95 = bf16[4,4,2048]{2,1,0:T(4,128)(2,1)} reshape(bf16[4,4,2,8,128]{4,3,2,1,0:T(8,128)(2,1)S(1)} %copy.22) | data formatting | bytes 131072 | tf_op jit(solution)/shard_map/reshape | solution.py:293
  (10 shorter events, 0.1 us)
Async XLA Ops:
  0.9 12.9 %collective-permute-start = (bf16[256,128]{1,0:T(8,128)(2,1)S(1)}, bf16[256,128]{1,0:T(8,128)(2,1)S(1)}, u32[]{:S(2)}, u32[]{:S(2)}) collective-permute-start(bf16[256,128]{1,0:T(8,128)(2,1)S(1)} %bitcast.25), channel_id=1, source_target_pairs={{0,2},{2,0},{4,6},{6,4},{8,10},{10,8},{12,14},{14,12},{1,3},{3,1},... | collective-permute-start | bytes 196616 | tf_op jit(solution)/shard_map/ppermute | solution.py:216
  12.1 12.1 %copy-start = (f32[8192]{0:T(1024)S(1)}, f32[8192]{0:T(1024)}, u32[]{:S(2)}) copy-start(f32[8192]{0:T(1024)} %convert_element_type.19) | copy-start | bytes 98308
  13.8 7.7 %collective-permute-start.1 = (bf16[512,128]{1,0:T(8,128)(2,1)S(1)}, bf16[512,128]{1,0:T(8,128)(2,1)S(1)}, u32[]{:S(2)}, u32[]{:S(2)}) collective-permute-start(bf16[512,128]{1,0:T(8,128)(2,1)S(1)} %pad_maximum_fusion.1), channel_id=1, source_target_pairs={{0,4},{2,6},{4,0},{6,2},{8,12},{10,14},{12,8},{14,10},{1,5},{3,7},... | collective-permute-start | bytes 393224 | tf_op jit(solution)/shard_map/ppermute | solution.py:216
  21.5 17.8 %collective-permute-start.2 = (bf16[1024,128]{1,0:T(8,128)(2,1)S(1)}, bf16[1024,128]{1,0:T(8,128)(2,1)S(1)}, u32[]{:S(2)}, u32[]{:S(2)}) collective-permute-start(bf16[1024,128]{1,0:T(8,128)(2,1)S(1)} %pad_maximum_fusion), channel_id=1, source_target_pairs={{0,8},{2,10},{4,12},{6,14},{8,0},{10,2},{12,4},{14,6},{1,9},{3,11}... | collective-permute-start | bytes 786440 | tf_op jit(solution)/shard_map/ppermute | solution.py:216

commit v4 on v3

--- a/solution.py
+++ b/solution.py
@@ -14,6 +14,8 @@
 norm_epsilon = 1e-05
 VMEM_LIMIT = 48 * 1024 * 1024
 UNROLL = 8
+ROW_BITS = 16
+ROW_MASK = (1 << ROW_BITS) - 1
 
 
 def vmem():
@@ -34,7 +36,8 @@
 
 
 def attend_kernel(
-    rows_dev, n, pieces, rows_ref, counts_ref, lookup_ref, pool, prompt_k, prompt_v, fresh, *others
+    rows_dev, n, pieces, found_ref, dest_ref, joined_ref, done_ref, pool, prompt_k, prompt_v, fresh,
+    *others
 ):
     blocks = others[:pieces]
     out_ref, ml_ref, q_ref, acc, tops, totals = others[pieces:]
@@ -63,6 +66,12 @@
     twice = jnp.where(lax.rem(lane, 2) == 0, lane // 2, page_len)
     contract_last = (((1,), (1,)), ((), ()))
 
+    me = lax.axis_index("section")
+    steps = fresh.shape[0] // (2 * rows_dev)
+    fresh_kv = jnp.concatenate(
+        [fresh[...], jnp.zeros((wide - fresh.shape[0], 2 * HS), fresh.dtype)], axis=0
+    )
+
     def load_pair(ref, at):
         return ref[pl.ds(pl.multiple_of(at * wide, wide), wide), :]
 
@@ -72,14 +81,20 @@
 
     def page_part(place, count, pages, at, kind):
         q = q_ref[pl.ds(pl.multiple_of(place * span, span), span), :]
-        kv = load_split(pages, at) if kind == "split" else load_pair(pages, at)
+        if kind == "split":
+            kv = load_split(pages, at)
+        elif kind == "fresh":
+            kv = fresh_kv
+        else:
+            kv = load_pair(pages, at)
         scores = lax.dot_general(
             q, kv, contract_last, preferred_element_type=jnp.float32
         ) * scale
         if kind == "split":
             usable = lane < count
         elif kind == "fresh":
-            usable = twice <= step
+            since = twice - at * steps
+            usable = (since >= 0) & (since <= step)
         else:
             usable = twice < count
         scores = jnp.where(usable, scores, masked_value)
@@ -109,25 +124,38 @@
         totals[place, :] = totals[place, :] * keep + total * add
         acc[place, :] = acc[place, :] * keep + summed * add
 
-    def run(first, count, pages, kind):
+    def pool_place(at):
+        packed = found_ref[at]
+        return jnp.bitwise_and(packed, ROW_MASK), jnp.right_shift(packed, ROW_BITS)
+
+    def prompt_place(at):
+        page = me * prompt_pages + at
+        count = jnp.where(done_ref[page] == 1, page_len, 0)
+        return dest_ref[page] * rows_dev + joined_ref[page], count
+
+    def fresh_place(at):
+        return me * rows_dev + at, steps
+
+    def run(where, count, pages, kind):
         many = math.gcd(count, UNROLL)
 
         def some(i, _):
             parts = []
             for u in range(many):
                 at = i * many + u
-                row = rows_ref[first + at]
-                place = lookup_ref[first + at]
-                parts.append((row, page_part(place, counts_ref[first + at], pages, at, kind)))
+                row, live = where(at)
+                owner = row // rows_dev
+                place = jnp.bitwise_xor(me, owner) * rows_dev + (row - owner * rows_dev)
+                parts.append((row, page_part(place, live, pages, at, kind)))
             for row, part in parts:
                 update(row, part)
             return 0
 
         lax.fori_loop(0, count // many, some, 0)
 
-    run(0, pool_pages, pool, "pair")
-    run(pool_pages, prompt_pages, (prompt_k, prompt_v), "split")
-    run(pool_pages + prompt_pages, rows_dev, fresh, "fresh")
+    run(pool_place, pool_pages, pool, "pair")
+    run(prompt_place, prompt_pages, (prompt_k, prompt_v), "split")
+    run(fresh_place, rows_dev, None, "fresh")
 
     block = rows_dev * span
     lane = lax.broadcasted_iota(jnp.int32, (block, HS), 1)
@@ -239,24 +267,9 @@
         page_len,
     )
     row_ids = jnp.arange(all_rows, dtype=jnp.int32)
-    packed = token_fill * all_rows + row_ids[:, None]
+    packed = token_fill * (1 << ROW_BITS) + row_ids[:, None]
     found = jnp.sum(jnp.where(page_hits, packed[:, :, None], 0), axis=(0, 1))
-    own_pages = me * prompt_pages
-    dest = lax.dynamic_slice_in_dim(ship_dest[:, 0], own_pages, prompt_pages, 0)
-    joined = lax.dynamic_slice_in_dim(page_row, own_pages, prompt_pages, 0)
-    done = lax.dynamic_slice_in_dim(finished, own_pages, prompt_pages, 0)
-    own_rows = me * rows_dev + jnp.arange(rows_dev, dtype=jnp.int32)
-    rows = jnp.concatenate([found % all_rows, dest * rows_dev + joined, own_rows])
-    lookup = (me ^ (rows // rows_dev)) * rows_dev + rows % rows_dev
-    counts = jnp.concatenate(
-        [
-            found // all_rows,
-            jnp.where(done == 1, page_len, 0).astype(jnp.int32),
-            jnp.zeros((rows_dev,), jnp.int32),
-        ]
-    )
-    fresh = jnp.pad(new_kv, ((0, 0), (0, page_len - steps), (0, 0), (0, 0)))
-    fresh = fresh.reshape(rows_dev * page_len * 2, width_kv)
+    fresh = new_kv.reshape(rows_dev * steps * 2, width_kv)
 
     parts, mls = pl.pallas_call(
         functools.partial(attend_kernel, rows_dev, n, len(blocks)),
@@ -264,13 +277,13 @@
             jax.ShapeDtypeStruct((n, block, HS), jnp.bfloat16),
             jax.ShapeDtypeStruct((n, 8, block), jnp.float32),
         ),
-        in_specs=[smem()] * 3 + [vmem()] * (4 + len(blocks)),
+        in_specs=[smem()] * 4 + [vmem()] * (4 + len(blocks)),
         out_specs=(vmem(), vmem()),
         scratch_shapes=[pltpu.VMEM((n * block, 2 * HS), jnp.bfloat16)]
         + [pltpu.VMEM((n * block, HS), jnp.float32)] * 3,
         compiler_params=pltpu.CompilerParams(vmem_limit_bytes=VMEM_LIMIT),
     )(
-        rows, counts, lookup, pool, prompt_kv[0], prompt_kv[1], fresh, *blocks,
+        found, ship_dest.reshape(-1), page_row, finished, pool, prompt_kv[0], prompt_kv[1], fresh, *blocks,
     )
 
     merged = pl.pallas_call(

time: 65.4 us -> 61.4 us (0.939)
  other arithmetic: 11.8 us -> 9.56 us
  local copies, waits for them, and re-layouts: 8.26 us -> 6.39 us
    pad x1 -> x0, local copies, waits for them, and re-layouts: 1.54 us -> none  [body(): fresh = jnp.pad(new_kv, ((0, 0), (0, page_len - steps), (0, 0), (0, 0)))]
    add x4 -> x1, other arithmetic: 1.57 us -> 0.73 us  [body(): packed = token_fill * (1 << ROW_BITS) + row_ids[:, None]]
    select_n x2 -> x0, other arithmetic: 0.75 us -> none  [the longest x1 0.74 us: body(): jnp.where(done == 1, page_len, 0).astype(jnp.int32)]
  transfers between devices with their start and end apart: 3 -> 3, of which waited for: 0 -> 0; matrix products, arithmetic and copies ran while one was open for 52% -> 48% of each run, Pallas kernels for 0% -> 0%
where the time goes in v4:
time: 61.4 us; the launch traced here: 61 us
  Pallas kernels  25.1 us (41%)
  matrix products  15 us (24%)
  other arithmetic  9.56 us (16%)
  local copies, waits for them, and re-layouts  6.39 us (10%)
  starting transfers between devices  4.75 us (8%)
    pallas_call x1, Pallas kernels, body(): pl.pallas_call(functools.partial(merge_kernel, n), out_shape=jax.ShapeDty...  16.2 us
    dot_general x1, matrix products, body(): jnp.einsum('td,dkc->ktc', normed, w_kv, preferred_element_type=jnp.float32)  15 us
    pallas_call x1, Pallas kernels, body(): pl.pallas_call(functools.partial(attend_kernel, rows_dev, n, len(blocks))...  8.89 us
    reduce_sum x1, other arithmetic, row_spread(): jnp.mean(states * states, axis=-1, keepdims=True) + norm_epsilon  7.18 us
    ppermute x3, starting transfers between devices, body(): other = lax.ppermute(whole, 'section', [(i, i ^ size) for i in range(n)])  4.75 us
    reshape x1, local copies, waits for them, and re-layouts, body(): pool = pool_cache.reshape(pool_pages * page_len * 2, width_kv)  4.03 us
  transfers between devices with their start and end apart: 3, of which 0 were waited for; matrix products, arithmetic and copies ran while one was open for 48% of the time, Pallas kernels for 0%

profile of v4, /device:TPU:8, one launch (start us, length us, event | category | flops | bytes accessed | tf_op | source)
XLA Modules:
  0.0 61.0 jit_solution(11008330412153996805)
XLA Ops:
  0.0 0.9 %reshape.91 = bf16[4,4,2,8,128]{4,3,2,1,0:T(8,128)(2,1)S(1)} reshape(bf16[4,4,2048]{2,1,0:T(4,128)(2,1)} %param.15) | data formatting | bytes 131072 | tf_op jit(solution)/shard_map/reshape | solution.py:235
  0.9 1.6 %collective-permute-start = (bf16[256,128]{1,0:T(8,128)(2,1)S(1)}, bf16[256,128]{1,0:T(8,128)(2,1)S(1)}, u32[]{:S(2)}, u32[]{:S(2)}) collective-permute-start(bf16[256,128]{1,0:T(8,128)(2,1)S(1)} %bitcast.24), channel_id=1, source_target_pairs={{0,2},{2,0},{4,6},{6,4},{8,10},{10,8},{12,14},{14,12},{1,3},{3,1},... | collective-permute-start | bytes 196616 | tf_op jit(solution)/shard_map/ppermute | solution.py:244
  2.5 4.0 %reshape.93.pool = bf16[6144,256]{1,0:T(8,128)(2,1)S(1)} reshape(bf16[48,64,2,256]{3,2,1,0:T(2,128)(2,1)} %param.14) | data formatting | bytes 6291456 | tf_op jit(solution)/shard_map/reshape | solution.py:238
  6.5 0.7 %convert_element_type.17 = f32[8192]{0:T(1024)S(1)} convert(bf16[8192]{0:T(1024)(128)(2,1)} %param.12) | non-fusion elementwise | flops 8192 | bytes 49152 | tf_op jit(solution)/shard_map/convert_element_type | solution.py:257
  7.3 0.7 %reshape.94.fresh = bf16[32,256]{1,0:T(8,128)(2,1)S(1)} reshape(bf16[4,4,2,256]{3,2,1,0:T(2,128)(2,1)} %param.16) | data formatting | bytes 32768 | tf_op jit(solution)/shard_map/reshape | solution.py:272
  8.0 0.7 %iota_add_fusion = s32[32,12]{0,1:T(8,128)S(1)} fusion(s32[12]{0:T(128)S(1)} %iota_multiply_fusion, s32[32]{0:T(128)} %param.21), kind=kLoop, calls=%fused_computation.15 | loop fusion | flops 1536 | bytes 1712 | tf_op jit(solution)/shard_map/add | solution.py:270
  8.7 0.9 %select_reduce_fusion.found_ref = s32[48]{0:T(128)S(1)} fusion(s32[32,12]{0,1:T(8,128)S(1)} %iota_add_fusion, s32[48]{0:T(128)S(1)} %iota_add_fusion.1, s32[32,12]{0,1:T(8,128)} %param.20), kind=kLoop, calls=%fused_computation.13 | loop fusion | flops 55248 | bytes 3456 | tf_op jit(solution)/shard_map/reduce_sum | solution.py:271
  9.6 0.0 collective-permute-done.others_1_
  9.6 0.5 collective-permute-start.1
  10.1 7.2 %fusion = f32[1024]{0:T(1024)S(1)} fusion(bf16[1024,8192]{1,0:T(8,128)(2,1)} %param.11), kind=kLoop, calls=%fused_computation.2 | loop fusion | flops 25164800 | bytes 16781312 | tf_op jit(solution)/shard_map/reduce_sum | solution.py:208
  17.3 0.0 collective-permute-done.1.others_2_
  17.4 2.7 %collective-permute-start.2 = (bf16[1024,128]{1,0:T(8,128)(2,1)S(1)}, bf16[1024,128]{1,0:T(8,128)(2,1)S(1)}, u32[]{:S(2)}, u32[]{:S(2)}) collective-permute-start(bf16[1024,128]{1,0:T(8,128)(2,1)S(1)} %pad_maximum_fusion), channel_id=1, source_target_pairs={{0,8},{2,10},{4,12},{6,14},{8,0},{10,2},{12,4},{14,6},{1,9},{3,11}... | collective-permute-start | bytes 786440 | tf_op jit(solution)/shard_map/ppermute | solution.py:244
  20.0 0.0 copy-start
  20.0 0.0 copy-start.1
  20.0 0.0 copy-start.2
  20.0 15.0 %fusion.12 = bf16[2,1024,256]{2,1,0:T(8,128)(2,1)S(1)} fusion(bf16[8192,2,256]{2,1,0:T(2,128)(2,1)} %param.13, bf16[1024,8192]{1,0:T(8,128)(2,1)} %param.11, f32[8192]{0:T(1024)S(1)} %convert_element_type.17, f32[1024]{0:T(1024)S(1)} %add_rsqrt_fusion), kind=kOutput, calls=%fused_computation.9 | convolution fusion | flops 8624013312 | bytes 26251264 | tf_op jit(solution)/shard_map/td,dkc->ktc/dot_general | solution.py:258
  35.1 0.1 slice_bitcast_fusion
  35.2 0.0 collective-permute-done.2.others_3_
  35.2 0.0 copy-done
  35.2 0.0 copy-done.1
  35.2 0.0 copy-done.2
  35.2 8.9 %shard_map.109 = (bf16[8,256,128]{2,1,0:T(8,128)(2,1)S(1)}, f32[8,8,256]{2,1,0:T(8,128)S(1)}) custom-call(s32[48]{0:T(128)S(1)} %select_reduce_fusion.found_ref, s32[128]{0:T(128)S(1)} %bitcast.29, s32[128]{0:T(128)S(1)} %copy-done.1, s32[128]{0:T(128)S(1)} %copy-done.2, bf16[6144,256]{1,0:T(8,128)(2,1)S(1)} %reshape.93.pool, ...), custom_call_target="tpu_custom_call" | custom-call | tf_op jit(solution)/shard_map/pallas_call | solution.py:274
  44.1 16.2 %shard_map.110 = bf16[256,128]{1,0:T(8,128)(2,1)S(1)} custom-call(bf16[8,256,128]{2,1,0:T(8,128)(2,1)S(1)} %get-tuple-element.17.part_ref, f32[8,8,256]{2,1,0:T(8,128)S(1)} %get-tuple-element.18.ml_ref), custom_call_target="tpu_custom_call" | custom-call | tf_op jit(solution)/shard_map/pallas_call | solution.py:289
  60.4 0.6 %reshape.96 = bf16[4,4,2048]{2,1,0:T(4,128)(2,1)} reshape(bf16[4,4,2,8,128]{4,3,2,1,0:T(8,128)(2,1)S(1)} %copy.22) | data formatting | bytes 131072 | tf_op jit(solution)/shard_map/reshape | solution.py:306
  (7 shorter events, 0.1 us)
Async XLA Ops:
  0.9 8.7 %collective-permute-start = (bf16[256,128]{1,0:T(8,128)(2,1)S(1)}, bf16[256,128]{1,0:T(8,128)(2,1)S(1)}, u32[]{:S(2)}, u32[]{:S(2)}) collective-permute-start(bf16[256,128]{1,0:T(8,128)(2,1)S(1)} %bitcast.24), channel_id=1, source_target_pairs={{0,2},{2,0},{4,6},{6,4},{8,10},{10,8},{12,14},{14,12},{1,3},{3,1},... | collective-permute-start | bytes 196616 | tf_op jit(solution)/shard_map/ppermute | solution.py:244
  9.6 7.7 %collective-permute-start.1 = (bf16[512,128]{1,0:T(8,128)(2,1)S(1)}, bf16[512,128]{1,0:T(8,128)(2,1)S(1)}, u32[]{:S(2)}, u32[]{:S(2)}) collective-permute-start(bf16[512,128]{1,0:T(8,128)(2,1)S(1)} %pad_maximum_fusion.1), channel_id=1, source_target_pairs={{0,4},{2,6},{4,0},{6,2},{8,12},{10,14},{12,8},{14,10},{1,5},{3,7},... | collective-permute-start | bytes 393224 | tf_op jit(solution)/shard_map/ppermute | solution.py:244
  17.4 17.8 %collective-permute-start.2 = (bf16[1024,128]{1,0:T(8,128)(2,1)S(1)}, bf16[1024,128]{1,0:T(8,128)(2,1)S(1)}, u32[]{:S(2)}, u32[]{:S(2)}) collective-permute-start(bf16[1024,128]{1,0:T(8,128)(2,1)S(1)} %pad_maximum_fusion), channel_id=1, source_target_pairs={{0,8},{2,10},{4,12},{6,14},{8,0},{10,2},{12,4},{14,6},{1,9},{3,11}... | collective-permute-start | bytes 786440 | tf_op jit(solution)/shard_map/ppermute | solution.py:244
  20.0 15.1 %copy-start = (s32[128,1]{0,1:T(1,128)S(1)}, s32[128,1]{0,1:T(1,128)}, u32[]{:S(2)}) copy-start(s32[128,1]{0,1:T(1,128)} %param.17) | copy-start | bytes 1540
  20.0 15.2 %copy-start.1 = (s32[128]{0:T(128)S(1)}, s32[128]{0:T(128)}, u32[]{:S(2)}) copy-start(s32[128]{0:T(128)} %joined_ref.1) | copy-start | bytes 1540
  20.0 15.2 %copy-start.2 = (s32[128]{0:T(128)S(1)}, s32[128]{0:T(128)}, u32[]{:S(2)}) copy-start(s32[128]{0:T(128)} %done_ref.1) | copy-start | bytes 1540

commit v5 on v4

--- a/solution.py
+++ b/solution.py
@@ -54,7 +54,7 @@
         start += size
     page_len = 64
     wide = 2 * page_len
-    pool_pages = pool.shape[0] // wide
+    pool_pages = pool.shape[0]
     prompt_pages = prompt_k.shape[0] // page_len
     scale = 1.0 / math.sqrt(HS)
     acc[...] = jnp.zeros_like(acc)
@@ -73,7 +73,7 @@
     )
 
     def load_pair(ref, at):
-        return ref[pl.ds(pl.multiple_of(at * wide, wide), wide), :]
+        return ref[at].reshape(wide, 2 * HS)
 
     def load_split(refs, at):
         here = pl.ds(pl.multiple_of(at * page_len, page_len), page_len)
@@ -235,7 +235,7 @@
     own_q = queries.reshape(rows_dev, steps, kv_heads, group, HS).transpose(0, 2, 1, 3, 4)
     own_q = own_q.reshape(block, HS)
     blocks = [own_q]
-    pool = pool_cache.reshape(pool_pages * page_len * 2, width_kv)
+    pool = pool_cache
     prompts = prompt_states
     spread = None
     size = 1

time: 61.4 us -> 57.6 us (0.938)
  local copies, waits for them, and re-layouts: 6.39 us -> 2.37 us
    reshape x1 -> x0, local copies, waits for them, and re-layouts: 4.03 us -> none  [body(): pool = pool_cache.reshape(pool_pages * page_len * 2, width_kv)]
  transfers between devices with their start and end apart: 3 -> 3, of which waited for: 0 -> 0; matrix products, arithmetic and copies ran while one was open for 48% -> 45% of each run, Pallas kernels for 0% -> 0%
where the time goes in v5:
time: 57.6 us; the launch traced here: 57.2 us
  Pallas kernels  25.2 us (44%)
  matrix products  15.1 us (26%)
  other arithmetic  9.56 us (17%)
  starting transfers between devices  4.75 us (8%)
  local copies, waits for them, and re-layouts  2.37 us (4%)
    pallas_call x1, Pallas kernels, body(): pl.pallas_call(functools.partial(merge_kernel, n), out_shape=jax.ShapeDty...  16.2 us
    dot_general x1, matrix products, body(): jnp.einsum('td,dkc->ktc', normed, w_kv, preferred_element_type=jnp.float32)  15.1 us
    pallas_call x1, Pallas kernels, body(): pl.pallas_call(functools.partial(attend_kernel, rows_dev, n, len(blocks))...  9.01 us
    reduce_sum x1, other arithmetic, row_spread(): jnp.mean(states * states, axis=-1, keepdims=True) + norm_epsilon  7.18 us
    ppermute x3, starting transfers between devices, body(): other = lax.ppermute(whole, 'section', [(i, i ^ size) for i in range(n)])  4.75 us
  transfers between devices with their start and end apart: 3, of which 0 were waited for; matrix products, arithmetic and copies ran while one was open for 45% of the time, Pallas kernels for 0%

profile of v5, /device:TPU:8, one launch (start us, length us, event | category | flops | bytes accessed | tf_op | source)
XLA Modules:
  0.0 57.2 jit_solution(17284204124339084726)
XLA Ops:
  0.0 0.9 %reshape.88 = bf16[4,4,2,8,128]{4,3,2,1,0:T(8,128)(2,1)S(1)} reshape(bf16[4,4,2048]{2,1,0:T(4,128)(2,1)} %param.15) | data formatting | bytes 131072 | tf_op jit(solution)/shard_map/reshape | solution.py:235
  0.9 1.6 %collective-permute-start = (bf16[256,128]{1,0:T(8,128)(2,1)S(1)}, bf16[256,128]{1,0:T(8,128)(2,1)S(1)}, u32[]{:S(2)}, u32[]{:S(2)}) collective-permute-start(bf16[256,128]{1,0:T(8,128)(2,1)S(1)} %bitcast.24), channel_id=1, source_target_pairs={{0,2},{2,0},{4,6},{6,4},{8,10},{10,8},{12,14},{14,12},{1,3},{3,1},... | collective-permute-start | bytes 196616 | tf_op jit(solution)/shard_map/ppermute | solution.py:244
  2.5 0.7 %convert_element_type.17 = f32[8192]{0:T(1024)S(1)} convert(bf16[8192]{0:T(1024)(128)(2,1)} %param.12) | non-fusion elementwise | flops 8192 | bytes 49152 | tf_op jit(solution)/shard_map/convert_element_type | solution.py:257
  3.2 0.7 %reshape.90.fresh = bf16[32,256]{1,0:T(8,128)(2,1)S(1)} reshape(bf16[4,4,2,256]{3,2,1,0:T(2,128)(2,1)} %param.16) | data formatting | bytes 32768 | tf_op jit(solution)/shard_map/reshape | solution.py:272
  4.0 0.7 %iota_add_fusion = s32[32,12]{0,1:T(8,128)S(1)} fusion(s32[12]{0:T(128)S(1)} %iota_multiply_fusion, s32[32]{0:T(128)} %param.21), kind=kLoop, calls=%fused_computation.15 | loop fusion | flops 1536 | bytes 1712 | tf_op jit(solution)/shard_map/add | solution.py:270
  4.7 0.9 %select_reduce_fusion.found_ref = s32[48]{0:T(128)S(1)} fusion(s32[32,12]{0,1:T(8,128)S(1)} %iota_add_fusion, s32[48]{0:T(128)S(1)} %iota_add_fusion.1, s32[32,12]{0,1:T(8,128)} %param.20), kind=kLoop, calls=%fused_computation.13 | loop fusion | flops 55248 | bytes 3456 | tf_op jit(solution)/shard_map/reduce_sum | solution.py:271
  5.6 0.0 collective-permute-done.others_1_
  5.6 0.5 collective-permute-start.1
  6.1 7.2 %fusion = f32[1024]{0:T(1024)S(1)} fusion(bf16[1024,8192]{1,0:T(8,128)(2,1)} %param.11), kind=kLoop, calls=%fused_computation.2 | loop fusion | flops 25164800 | bytes 16781312 | tf_op jit(solution)/shard_map/reduce_sum | solution.py:208
  13.3 0.0 collective-permute-done.1.others_2_
  13.3 2.7 %collective-permute-start.2 = (bf16[1024,128]{1,0:T(8,128)(2,1)S(1)}, bf16[1024,128]{1,0:T(8,128)(2,1)S(1)}, u32[]{:S(2)}, u32[]{:S(2)}) collective-permute-start(bf16[1024,128]{1,0:T(8,128)(2,1)S(1)} %pad_maximum_fusion), channel_id=1, source_target_pairs={{0,8},{2,10},{4,12},{6,14},{8,0},{10,2},{12,4},{14,6},{1,9},{3,11}... | collective-permute-start | bytes 786440 | tf_op jit(solution)/shard_map/ppermute | solution.py:244
  16.0 0.0 copy-start
  16.0 0.0 copy-start.1
  16.0 0.0 copy-start.2
  16.0 0.0 copy-start.3
  16.0 15.1 %fusion.12 = bf16[2,1024,256]{2,1,0:T(8,128)(2,1)S(1)} fusion(bf16[8192,2,256]{2,1,0:T(2,128)(2,1)} %param.13, bf16[1024,8192]{1,0:T(8,128)(2,1)} %param.11, f32[8192]{0:T(1024)S(1)} %convert_element_type.17, f32[1024]{0:T(1024)S(1)} %add_rsqrt_fusion), kind=kOutput, calls=%fused_computation.9 | convolution fusion | flops 8624013312 | bytes 26251264 | tf_op jit(solution)/shard_map/td,dkc->ktc/dot_general | solution.py:258
  31.2 0.1 slice_bitcast_fusion
  31.2 0.0 collective-permute-done.2.others_3_
  31.3 0.0 copy-done
  31.3 0.0 copy-done.1
  31.3 0.0 copy-done.2
  31.3 0.0 copy-done.3
  31.3 9.0 %shard_map.109 = (bf16[8,256,128]{2,1,0:T(8,128)(2,1)S(1)}, f32[8,8,256]{2,1,0:T(8,128)S(1)}) custom-call(s32[48]{0:T(128)S(1)} %select_reduce_fusion.found_ref, s32[128]{0:T(128)S(1)} %bitcast.29, s32[128]{0:T(128)S(1)} %copy-done.2, s32[128]{0:T(128)S(1)} %copy-done.3, bf16[48,64,2,256]{3,2,1,0:T(2,128)(2,1)S(1)} %copy-done, ...), custom_call_target="tpu_custom_call" | custom-call | tf_op jit(solution)/shard_map/pallas_call | solution.py:274
  40.3 16.2 %shard_map.110 = bf16[256,128]{1,0:T(8,128)(2,1)S(1)} custom-call(bf16[8,256,128]{2,1,0:T(8,128)(2,1)S(1)} %get-tuple-element.17.part_ref, f32[8,8,256]{2,1,0:T(8,128)S(1)} %get-tuple-element.18.ml_ref), custom_call_target="tpu_custom_call" | custom-call | tf_op jit(solution)/shard_map/pallas_call | solution.py:289
  56.6 0.6 %reshape.92 = bf16[4,4,2048]{2,1,0:T(4,128)(2,1)} reshape(bf16[4,4,2,8,128]{4,3,2,1,0:T(8,128)(2,1)S(1)} %copy.22) | data formatting | bytes 131072 | tf_op jit(solution)/shard_map/reshape | solution.py:306
  (7 shorter events, 0.1 us)
Async XLA Ops:
  0.9 4.7 %collective-permute-start = (bf16[256,128]{1,0:T(8,128)(2,1)S(1)}, bf16[256,128]{1,0:T(8,128)(2,1)S(1)}, u32[]{:S(2)}, u32[]{:S(2)}) collective-permute-start(bf16[256,128]{1,0:T(8,128)(2,1)S(1)} %bitcast.24), channel_id=1, source_target_pairs={{0,2},{2,0},{4,6},{6,4},{8,10},{10,8},{12,14},{14,12},{1,3},{3,1},... | collective-permute-start | bytes 196616 | tf_op jit(solution)/shard_map/ppermute | solution.py:244
  5.6 7.7 %collective-permute-start.1 = (bf16[512,128]{1,0:T(8,128)(2,1)S(1)}, bf16[512,128]{1,0:T(8,128)(2,1)S(1)}, u32[]{:S(2)}, u32[]{:S(2)}) collective-permute-start(bf16[512,128]{1,0:T(8,128)(2,1)S(1)} %pad_maximum_fusion.1), channel_id=1, source_target_pairs={{0,4},{2,6},{4,0},{6,2},{8,12},{10,14},{12,8},{14,10},{1,5},{3,7},... | collective-permute-start | bytes 393224 | tf_op jit(solution)/shard_map/ppermute | solution.py:244
  13.3 17.9 %collective-permute-start.2 = (bf16[1024,128]{1,0:T(8,128)(2,1)S(1)}, bf16[1024,128]{1,0:T(8,128)(2,1)S(1)}, u32[]{:S(2)}, u32[]{:S(2)}) collective-permute-start(bf16[1024,128]{1,0:T(8,128)(2,1)S(1)} %pad_maximum_fusion), channel_id=1, source_target_pairs={{0,8},{2,10},{4,12},{6,14},{8,0},{10,2},{12,4},{14,6},{1,9},{3,11}... | collective-permute-start | bytes 786440 | tf_op jit(solution)/shard_map/ppermute | solution.py:244
  16.0 15.3 %copy-start = (bf16[48,64,2,256]{3,2,1,0:T(2,128)(2,1)S(1)}, bf16[48,64,2,256]{3,2,1,0:T(2,128)(2,1)}, u32[]{:S(2)}) copy-start(bf16[48,64,2,256]{3,2,1,0:T(2,128)(2,1)} %pool) | copy-start | bytes 9437188
  16.0 15.3 %copy-start.1 = (s32[128,1]{0,1:T(1,128)S(1)}, s32[128,1]{0,1:T(1,128)}, u32[]{:S(2)}) copy-start(s32[128,1]{0,1:T(1,128)} %param.17) | copy-start | bytes 1540
  16.0 15.3 %copy-start.2 = (s32[128]{0:T(128)S(1)}, s32[128]{0:T(128)}, u32[]{:S(2)}) copy-start(s32[128]{0:T(128)} %joined_ref.1) | copy-start | bytes 1540
  16.0 15.3 %copy-start.3 = (s32[128]{0:T(128)S(1)}, s32[128]{0:T(128)}, u32[]{:S(2)}) copy-start(s32[128]{0:T(128)} %done_ref.1) | copy-start | bytes 1540
